TPU v7x, 256 devices: a whole 4x4x8 slice. The times are simulated.
256 devices in a mesh: island: 8 (over z_hi, x), fsdp: 32 (over z_lo, y, core).
Axes of the slice: x: 4, y: 4, z: 8 (z_hi: 2, z_lo: 4; z = z_hi * 4 + z_lo), core: 2. Of those that a mesh axis runs over, the one named last changes fastest.
Arguments:
- normed: bfloat16 [8, 8192, 8192], P('island', 'fsdp'), may hold values from -6 to 6
- cotangent: bfloat16 [8, 8192, 512], P('island', 'fsdp'), may hold values from -6 to 6
- weights: float32 [8, 8192, 512], P('island', 'fsdp'), may hold values from -6 to 6
- first_moment: float32 [8, 8192, 512], P('island', 'fsdp'), may hold values from -6 to 6
- second_moment: float32 [8, 8192, 512], P('island', 'fsdp'), may hold values from 0.05 to 2
- outer_params: float32 [8192, 128], P(('fsdp', 'island')), may hold values from -6 to 6
- outer_momentum: float32 [8192, 128], P(('fsdp', 'island')), may hold values from -6 to 6
- fragment: int32 [1], replicated, may hold values from 0 to 384
Outputs:
- grad_input: bfloat16 [8, 8192, 8192], P('island', 'fsdp')
- new_weights: float32 [8, 8192, 512], P('island', 'fsdp')
- new_first: float32 [8, 8192, 512], P('island', 'fsdp')
- new_second: float32 [8, 8192, 512], P('island', 'fsdp')
- new_outer: float32 [8192, 128], P(('fsdp', 'island'))
- new_momentum: float32 [8192, 128], P(('fsdp', 'island'))
All inputs are finite; a program needn't handle non-finite values.
Results may differ from a plain program's by a relative error of at most 0.012.
Values may be sent and summed in bfloat16 or wider, within the bound.
No kernel may reach another device: no remote copies, remote signals or barrier semaphores. Data moves between devices by JAX's collectives and lax.ppermute only.
A program may use at most 128 MiB of HBM per device.

v0:
```python
import math

import jax
import jax.numpy as jnp
from jax import lax
from jax.sharding import PartitionSpec as P

BETA_FIRST = 0.9
BETA_SECOND = 0.95
EPSILON = 1e-08
INNER_RATE = 0.01
DECAY_RATE = 0.1
OUTER_RATE = 0.7
MOMENTUM = 0.9
MIX_WEIGHT = 0.5


def outer_update(outer_rows, momentum_rows, mean_rows):
    pseudo_grad = outer_rows - mean_rows
    momentum_next = MOMENTUM * momentum_rows + pseudo_grad
    outer_next = outer_rows - OUTER_RATE * (pseudo_grad + MOMENTUM * momentum_next)
    return (outer_next, momentum_next)


def local(
    normed, cotangent, weights, first_moment, second_moment, outer_params, outer_momentum, fragment
):
    tokens_in = normed[0]
    cotan = cotangent[0]
    master = weights[0]
    factor = 1.0 / math.sqrt(tokens_in.shape[1])
    w_half = master.astype(jnp.bfloat16)
    back_grad = (
        lax.dot_general(
            cotan,
            lax.all_gather(w_half, "fsdp", axis=0, tiled=True),
            (((1,), (1,)), ((), ())),
            preferred_element_type=jnp.float32,
        )
        * factor
    ).astype(jnp.bfloat16)
    gradient = lax.psum_scatter(
        (
            lax.dot_general(
                tokens_in, cotan, (((0,), (0,)), ((), ())), preferred_element_type=jnp.float32
            )
            * factor
        ).astype(jnp.bfloat16),
        "fsdp",
        scatter_dimension=0,
        tiled=True,
    ).astype(jnp.float32)
    moment_one = BETA_FIRST * first_moment[0] + (1.0 - BETA_FIRST) * gradient
    moment_two = BETA_SECOND * second_moment[0] + (1.0 - BETA_SECOND) * gradient * gradient
    stepped = master - INNER_RATE * (
        moment_one / (jnp.sqrt(moment_two) + EPSILON) + DECAY_RATE * master
    )
    head_width = outer_params.shape[1]
    offset = fragment[0]
    inner_frag = lax.dynamic_slice_in_dim(master, offset, head_width, 1)
    island_count = lax.axis_size("island")
    summed = lax.psum(inner_frag.astype(jnp.bfloat16), "island").astype(jnp.float32)
    outer_all, momentum_all = (
        lax.all_gather(outer_params, "island", axis=0, tiled=True),
        lax.all_gather(outer_momentum, "island", axis=0, tiled=True),
    )
    outer_rows_all, momentum_rows_all = outer_update(outer_all, momentum_all, summed / island_count)
    share_rows = outer_params.shape[0]
    row_start = lax.axis_index("island") * share_rows
    outer_next = lax.dynamic_slice_in_dim(outer_rows_all, row_start, share_rows, 0)
    momentum_next = lax.dynamic_slice_in_dim(momentum_rows_all, row_start, share_rows, 0)
    blended = (
        MIX_WEIGHT * lax.dynamic_slice_in_dim(stepped, offset, head_width, 1)
        + (1.0 - MIX_WEIGHT) * outer_rows_all
    )
    merged = lax.dynamic_update_slice_in_dim(stepped, blended, offset, 1)
    return (
        back_grad[None],
        merged[None],
        moment_one[None],
        moment_two[None],
        outer_next,
        momentum_next,
    )


def solution(mesh):
    return jax.shard_map(
        local,
        mesh=mesh,
        in_specs=(
            P("island", "fsdp", None),
            P("island", "fsdp", None),
            P("island", "fsdp", None),
            P("island", "fsdp", None),
            P("island", "fsdp", None),
            P(("fsdp", "island"), None),
            P(("fsdp", "island"), None),
            P(),
        ),
        out_specs=(
            P("island", "fsdp", None),
            P("island", "fsdp", None),
            P("island", "fsdp", None),
            P("island", "fsdp", None),
            P(("fsdp", "island"), None),
            P(("fsdp", "island"), None),
        ),
        check_vma=False,
    )
```

profile of v0, /device:TPU:1, one launch (start us, length us, event | category | flops | bytes accessed | tf_op | source)
XLA Modules:
  0.0 252.2 jit_solution(13587337637210078893)
XLA Ops:
  8.0 0.0 copy-start
  8.0 0.0 all-gather.2.cloned.1.call-start
  8.1 1.8 bitcast_convert_fusion
  9.9 0.0 all-gather.2.cloned.1.call-update
  9.9 0.0 reduce-scatter.2.cloned.1.call-start
  9.9 0.0 copy-done
  10.0 7.8 %multiply_convert_fusion = bf16[8192,512]{1,0:T(8,128)(2,1)} fusion(bf16[1,256,8192]{2,1,0:T(8,128)(2,1)} %param.8, bf16[1,256,512]{2,1,0:T(8,128)(2,1)S(1)} %copy-done), kind=kOutput, calls=%fused_computation | convolution fusion | flops 2155872256 | bytes 12845056 | tf_op jit(solution)/shard_map/dot_general | solution.py:44
  17.7 0.0 copy-start.1
  17.8 0.0 copy-start.5
  17.8 0.0 copy-start.6
  17.8 0.0 reduce-scatter.2.cloned.1.call-update
  17.8 0.0 copy-start.3
  17.8 0.0 copy-start.4
  17.8 0.0 all-reduce.2.cloned.1.call-start
  18.6 0.2 copy-done.1
  18.8 0.7 fusion.11
  19.5 0.0 all-reduce.2.cloned.1.call-update
  19.5 0.0 copy-done.5
  19.5 41.1 %all_gather.10 = f32[256,128]{1,0:T(8,128)S(1)} all-gather(f32[32,128]{1,0:T(8,128)S(1)} %copy-done.5), channel_id=1, replica_groups=mesh['island'=8,'fsdp'=32] {'island'}, dimensions={0}, use_global_device_ids=true | all-gather | bytes 147456 | tf_op jit(solution)/shard_map/all_gather | solution.py:64
  60.7 0.0 copy-done.6
  60.7 38.5 %all_gather.11 = f32[256,128]{1,0:T(8,128)S(1)} all-gather(f32[32,128]{1,0:T(8,128)S(1)} %copy-done.6), channel_id=1, replica_groups=mesh['island'=8,'fsdp'=32] {'island'}, dimensions={0}, use_global_device_ids=true | all-gather | bytes 147456 | tf_op jit(solution)/shard_map/all_gather | solution.py:65
  99.1 0.0 all-gather.2.cloned.1.call-done
  99.1 7.8 %fusion.1 = bf16[1,256,8192]{2,1,0:T(8,128)(2,1)} fusion(bf16[8192,512]{1,0:T(8,128)(2,1)} %all-gather.2.cloned.1.call-done, bf16[1,256,512]{2,1,0:T(8,128)(2,1)S(1)} %copy-done), kind=kOutput, calls=%fused_computation.3 | convolution fusion | flops 2151677952 | bytes 12845056 | tf_op jit(solution)/shard_map/dot_general | solution.py:34
  107.0 132.4 %reduce-scatter.2.cloned.1.call-done = bf16[256,512]{1,0:T(8,128)(2,1)} async-done(((bf16[8192,512]{1,0:T(8,128)(2,1)}), bf16[256,512]{1,0:T(8,128)(2,1)}) %reduce-scatter.2.cloned.1.call-update) | async-done | bytes 262160 | tf_op jit(solution)/shard_map/reduce_scatter | solution.py:42
  239.4 0.0 copy-done.3
  239.4 0.0 copy-done.4
  239.4 2.3 fusion.8
  241.7 0.0 all-reduce.2.cloned.1.call-done
  241.7 1.0 multiply_bitcast_fusion
  242.6 1.3 dynamic_update_slice.4
  244.0 0.0 copy-start.2
  244.0 0.7 constant_dynamic-slice_fusion
  244.7 0.1 copy-done.2
Async XLA Ops:
  8.0 1.9 copy-start
  8.0 91.1 %all-gather.2.cloned.1.call-start = ((), (), s32[]{:S(2)}) async-start(), calls=%async_computation.1 | async-start | bytes 8650752 | tf_op jit(solution)/shard_map/all_gather | solution.py:36
  9.9 229.5 %reduce-scatter.2.cloned.1.call-start = ((), (), s32[]{:S(2)}) async-start(), calls=%async_computation.2 | async-start | bytes 8650752 | tf_op jit(solution)/shard_map/reduce_scatter | solution.py:42
  17.7 1.0 copy-start.1
  17.8 1.8 copy-start.5
  17.8 42.9 %copy-start.6 = (f32[32,128]{1,0:T(8,128)S(1)}, f32[32,128]{1,0:T(8,128)}, u32[]{:S(2)}) copy-start(f32[32,128]{1,0:T(8,128)} %param.14) | copy-start | bytes 49156
  17.8 221.6 %copy-start.3 = (f32[1,256,512]{2,1,0:T(8,128)S(1)}, f32[1,256,512]{2,1,0:T(8,128)}, u32[]{:S(2)}) copy-start(f32[1,256,512]{2,1,0:T(8,128)} %param.12) | copy-start | bytes 1572868
  17.8 221.6 %copy-start.4 = (f32[1,256,512]{2,1,0:T(8,128)S(1)}, f32[1,256,512]{2,1,0:T(8,128)}, u32[]{:S(2)}) copy-start(f32[1,256,512]{2,1,0:T(8,128)} %param.11) | copy-start | bytes 1572868
  17.8 223.9 %all-reduce.2.cloned.1.call-start = ((), (), s32[]{:S(2)}) async-start(), calls=%async_computation.3 | async-start | bytes 131072 | tf_op jit(solution)/shard_map/psum | solution.py:62
  244.0 0.8 copy-start.2
Sparse Core Ops, SparseCore 0:
  11.3 73.9 all-gather.1
  87.8 151.5 reduce-scatter.1
Sparse Core Ops, SparseCore 1:
  20.9 106.1 all-reduce.1
where the time goes:
time: 257 us; the launch traced here: 252 us
  waiting for transfers between devices  132 us (51%)
  blocking collectives  79.6 us (31%)
  between operations  16.3 us (6%)
  matrix products  15.6 us (6%)
  other arithmetic  5.05 us (2%)
  local copies, waits for them, and re-layouts  3.06 us (1%)
    reduce_scatter x1, waiting for transfers between devices, local(): lax.psum_scatter((lax.dot_general(tokens_in, cotan, (((0,), (0,)), ((), (...  132 us
    all_gather x1, blocking collectives, local(): lax.all_gather(outer_params, 'island', axis=0, tiled=True)  41.1 us
    all_gather x1, blocking collectives, local(): lax.all_gather(outer_momentum, 'island', axis=0, tiled=True)  38.5 us
    dot_general x1, matrix products, local(): lax.dot_general(cotan, lax.all_gather(w_half, 'fsdp', axis=0, tiled=True)...  7.83 us
    dot_general x1, matrix products, local(): lax.dot_general(tokens_in, cotan, (((0,), (0,)), ((), ())), preferred_ele...  7.79 us
  transfers between devices with their start and end apart: 3, of which 1 were waited for; matrix products, arithmetic and copies ran while one was open for 7% of the time, Pallas kernels for 0%

commit v1 on v0

v1 whole, which is shorter than its diff:
```python
import math

import jax
import jax.numpy as jnp
from jax import lax
from jax.experimental import pallas as pl
from jax.experimental.pallas import tpu as pltpu
from jax.sharding import PartitionSpec as P

BETA_FIRST = 0.9
BETA_SECOND = 0.95
EPSILON = 1e-08
INNER_RATE = 0.01
DECAY_RATE = 0.1
OUTER_RATE = 0.7
MOMENTUM = 0.9
MIX_WEIGHT = 0.5

NZ, NY, NC = 4, 4, 2
NX = 4
F32, BF16 = jnp.float32, jnp.bfloat16
COST = pl.CostEstimate(flops=1, bytes_accessed=1, transcendentals=0)
VMEM_LIMIT = 8 * 1024 * 1024

SMEM_SPEC = pl.BlockSpec(memory_space=pltpu.SMEM)
VMEM_SPEC = pl.BlockSpec(memory_space=pltpu.VMEM)
ANY_SPEC = pl.BlockSpec(memory_space=pl.ANY)


def fsdp_perm(move):
    pairs = []
    for z in range(NZ):
        for y in range(NY):
            for c in range(NC):
                tz, ty, tc = move(z, y, c)
                pairs.append(((z * NY + y) * NC + c, ((tz % NZ) * NY + ty % NY) * NC + tc))
    return pairs


def turned_perms(move):
    return [fsdp_perm(lambda z, y, c, k=k: move(z, y, c, k if c == 0 else -k)) for k in (1, -1)]


ON_Y, BACK_Y = turned_perms(lambda z, y, c, k: (z, y + k, c))
ON_Z, BACK_Z = turned_perms(lambda z, y, c, k: (z + k, y, c))
SWAP = fsdp_perm(lambda z, y, c: (z, y, 1 - c))


def island_perm(move):
    pairs = []
    for h in range(2):
        for x in range(NX):
            th, tx = move(h, x)
            pairs.append((h * NX + x, th * NX + tx))
    return pairs


PAIR_X = island_perm(lambda h, x: (h, x ^ 1))
CROSS_X = island_perm(lambda h, x: (h, 3 - x))
SWAP_H = island_perm(lambda h, x: (1 - h, x))


def params():
    return pltpu.CompilerParams(vmem_limit_bytes=VMEM_LIMIT)


def halve(master):
    def body(master, out):
        out[...] = master[...].astype(BF16)

    return pl.pallas_call(
        body,
        out_shape=jax.ShapeDtypeStruct(master.shape, BF16),
        in_specs=[VMEM_SPEC],
        out_specs=VMEM_SPEC,
        compiler_params=params(),
        cost_estimate=COST,
    )(master)


def pack(table, groups, normed, cotan, rows):
    tokens, kvw = cotan.shape
    halves = kvw // rows
    extra = [halves] + [0] * (len(groups) - 2) + [halves]

    def body(table, normed, cotan, *outs):
        for h in range(halves):
            turned = cotan[:, h * rows : (h + 1) * rows].T
            for i in (0, len(groups) - 1):
                outs[i][len(groups[i]) + h] = turned
        for out, places in zip(outs, groups):
            for j, place in enumerate(places):
                cols = pl.ds(pl.multiple_of(table[place] * rows, rows), rows)
                out[j] = normed[:, cols]

    return pl.pallas_call(
        body,
        out_shape=[
            jax.ShapeDtypeStruct((len(g) + n, tokens, rows), BF16) for g, n in zip(groups, extra)
        ],
        in_specs=[SMEM_SPEC] + [VMEM_SPEC] * 2,
        out_specs=[VMEM_SPEC] * len(groups),
        compiler_params=params(),
        cost_estimate=COST,
    )(table, normed, cotan)


def join(pieces):
    def body(*refs):
        at = 0
        for ref in refs[:-1]:
            refs[-1][pl.ds(at, ref.shape[0]), :] = ref[...]
            at += ref.shape[0]

    rows, columns = pieces[0].shape
    return pl.pallas_call(
        body,
        out_shape=jax.ShapeDtypeStruct((len(pieces) * rows, columns), pieces[0].dtype),
        in_specs=[VMEM_SPEC] * len(pieces),
        out_specs=VMEM_SPEC,
        compiler_params=params(),
        cost_estimate=COST,
    )(*pieces)


def grad_blocks(first, packed_first, groups, factor, own, swapped, packed):
    width = own.shape[2]
    halves = 2

    def body(own, swapped, packed, *outs):
        for group, out in enumerate(outs):
            for j in range(NZ):
                at = group * NZ + j
                for half in range(halves):
                    mine, theirs = own.shape[0] - halves + half, swapped.shape[0] - halves + half
                    total = jnp.dot(own[mine], own[first + at], preferred_element_type=F32)
                    total += jnp.dot(
                        swapped[theirs], packed[packed_first + at], preferred_element_type=F32
                    )
                    out[j, pl.ds(half * width, width), :] = (total * factor).astype(BF16)

    return pl.pallas_call(
        body,
        out_shape=[jax.ShapeDtypeStruct((NZ, halves * width, width), BF16)] * groups,
        in_specs=[VMEM_SPEC] * 3,
        out_specs=[VMEM_SPEC] * groups,
        compiler_params=params(),
        cost_estimate=COST,
    )(own, swapped, packed)


def add(*parts, split=False):
    blocks, *block = parts[0].shape

    def body(*refs):
        ins, outs = refs[: len(parts)], refs[len(parts) :]
        for j in range(blocks):
            total = ins[0][j].astype(F32)
            for ref in ins[1:]:
                total += ref[j].astype(F32)
            if split:
                outs[j][...] = total.astype(BF16)
            else:
                outs[0][j] = total.astype(BF16)

    shapes = [block] * blocks if split else [parts[0].shape]
    return pl.pallas_call(
        body,
        out_shape=[jax.ShapeDtypeStruct(tuple(shape), BF16) for shape in shapes],
        in_specs=[VMEM_SPEC] * len(parts),
        out_specs=[VMEM_SPEC] * len(shapes),
        compiler_params=params(),
        cost_estimate=COST,
    )(*parts)


def add_one(a, b):
    def body(a, b, out):
        out[...] = (a[...].astype(F32) + b[...].astype(F32)).astype(BF16)

    return pl.pallas_call(
        body,
        out_shape=jax.ShapeDtypeStruct(a.shape, BF16),
        in_specs=[VMEM_SPEC] * 2,
        out_specs=VMEM_SPEC,
        compiler_params=params(),
        cost_estimate=COST,
    )(a, b)


def input_blocks(table, entries, cotan, pieces, width, factor, dest=None):
    rows = width // (NZ * NY * NC)
    total = len(entries)
    operands = [table, cotan, *pieces]
    specs = [SMEM_SPEC] + [VMEM_SPEC] * (1 + len(pieces))
    aliases = {}
    if dest is not None:
        aliases = {len(operands): 0}
        operands.append(dest)
        specs.append(ANY_SPEC)

    def body(table, cotan, *refs):
        out, stage, sems = refs[-3:]
        copies = []
        for piece in refs[: len(pieces)]:
            for b in range(piece.shape[0] // rows):
                j = len(copies)
                block = piece[pl.ds(b * rows, rows), :]
                res = lax.dot_general(
                    cotan[...], block, (((1,), (1,)), ((), ())), preferred_element_type=F32
                )
                stage[j] = (res * factor).astype(BF16)
                cols = pl.ds(pl.multiple_of(table[entries[j]] * rows, rows), rows)
                copy = pltpu.make_async_copy(stage.at[j], out.at[:, cols], sems.at[j])
                copy.start()
                copies.append(copy)
        for copy in copies:
            copy.wait()

    return pl.pallas_call(
        body,
        out_shape=jax.ShapeDtypeStruct((cotan.shape[0], width), BF16),
        in_specs=specs,
        out_specs=ANY_SPEC,
        scratch_shapes=[
            pltpu.VMEM((total, cotan.shape[0], rows), BF16),
            pltpu.SemaphoreType.DMA((total,)),
        ],
        input_output_aliases=aliases,
        compiler_params=params(),
        cost_estimate=COST,
    )(*operands)


def mix_start(place, slope, islands, master, outer, momentum):
    rows, kvw = master.shape
    share, head = outer.shape

    def body(place, master, outer, momentum, out):
        turned = pltpu.roll(master[...], kvw - place[0], 1)
        out[...] = (slope / islands) * turned[:, :head]
        fixed = (1.0 - slope) * outer[...] - OUTER_RATE * MOMENTUM * MOMENTUM * momentum[...]
        own = pl.ds(pl.multiple_of(place[1], share), share)
        out[own, :] = out[own, :] + fixed

    return pl.pallas_call(
        body,
        out_shape=jax.ShapeDtypeStruct((rows, head), F32),
        in_specs=[SMEM_SPEC] + [VMEM_SPEC] * 3,
        out_specs=VMEM_SPEC,
        compiler_params=params(),
        cost_estimate=COST,
    )(place, master, outer, momentum)


def inner_step(place, slope, own, one, two, master, first, second, mix, outer, momentum):
    rows, kvw = master.shape
    share, head = outer.shape

    def body(place, own, one, two, master, first, second, mix, outer, momentum, *outs):
        w_out, f_out, s_out, o_out, m_out = outs
        gradient = (own[...].astype(F32) + (one[...].astype(F32) + two[...].astype(F32))).T
        weights = master[...]
        moment_one = BETA_FIRST * first[...] + (1.0 - BETA_FIRST) * gradient
        moment_two = BETA_SECOND * second[...] + (1.0 - BETA_SECOND) * gradient * gradient
        f_out[...] = moment_one
        s_out[...] = moment_two
        stepped = weights - INNER_RATE * (
            moment_one / (jnp.sqrt(moment_two) + EPSILON) + DECAY_RATE * weights
        )
        column = lax.broadcasted_iota(jnp.int32, stepped.shape, 1)
        inside = (column >= place[0]) & (column < place[0] + head)
        padding = jnp.zeros((rows, kvw - head), F32)
        placed = pltpu.roll(jnp.concatenate([mix[...], padding], axis=1), place[0], 1)
        w_out[...] = jnp.where(
            inside, MIX_WEIGHT * stepped + (1.0 - MIX_WEIGHT) * placed, stepped
        )
        fixed = (1.0 - slope) * outer[...] - OUTER_RATE * MOMENTUM * MOMENTUM * momentum[...]
        outer_next = mix[pl.ds(pl.multiple_of(place[1], share), share), :]
        o_out[...] = outer_next
        m_out[...] = MOMENTUM * momentum[...] + (outer[...] - (outer_next - fixed) / slope)

    return pl.pallas_call(
        body,
        out_shape=[jax.ShapeDtypeStruct(master.shape, F32)] * 3
        + [jax.ShapeDtypeStruct(outer.shape, F32)] * 2,
        in_specs=[SMEM_SPEC] + [VMEM_SPEC] * 9,
        out_specs=[VMEM_SPEC] * 5,
        compiler_params=params(),
        cost_estimate=COST,
    )(place, own, one, two, master, first, second, mix, outer, momentum)


def local(
    normed, cotangent, weights, first_moment, second_moment, outer_params, outer_momentum, fragment
):
    tokens_in, cotan, master = normed[0], cotangent[0], weights[0]
    rows, kvw = master.shape
    width = tokens_in.shape[1]
    factor = 1.0 / math.sqrt(width)
    me = lax.axis_index("fsdp")
    z, y, c = me // (NY * NC), (me // NC) % NY, me % NC

    def send(value, pairs, name):
        with jax.named_scope(name):
            return lax.ppermute(value, "fsdp", pairs)

    def send_island(value, pairs, name):
        with jax.named_scope(name):
            return lax.ppermute(value, "island", pairs)

    blocks = []
    for core, turn in ((c, 1 - 2 * c), (1 - c, 2 * c - 1)):
        for t in range(NY):
            for s in range(NZ):
                bz, by = (z - s * turn + NZ) % NZ, (y - t * turn + NY) % NY
                blocks.append((bz * NY + by) * NC + core)
    table = jnp.stack(blocks).astype(jnp.int32)

    def entry(core, t, s):
        return (core * NY + t % NY) * NZ + s % NZ

    def tie(*values):
        nonlocal table
        table, *tied = lax.optimization_barrier((table, *values))
        return tied[0] if len(tied) == 1 else tied

    islands = lax.axis_size("island")
    slope = OUTER_RATE * (1.0 + MOMENTUM)
    row_start = lax.axis_index("island") * outer_params.shape[0]
    place = jnp.stack([fragment[0], row_start.astype(jnp.int32)])

    order = (2, 1, 3, 0)
    first_places = [(2, s) for s in order]
    late_places = [(t, s) for t in (1, 3, 0) for s in order]

    def entries(core, places):
        return [entry(core, t, s) for t, s in places]

    swapping, swapping_late, own = tie(
        *pack(
            table,
            [
                entries(1, first_places),
                entries(1, late_places),
                entries(0, first_places + late_places),
            ],
            tokens_in,
            cotan,
            rows,
        )
    )
    swapped = send(swapping, SWAP, "swap_inputs")
    swapped_late = send(swapping_late, SWAP, "swap_inputs_late")
    w_half = tie(halve(tie(master)))
    za = send(w_half, ON_Z, "z_on")
    zb = send(w_half, BACK_Z, "z_back")

    swapped = tie(swapped)
    first = tie(*grad_blocks(0, 0, 1, factor, own, swapped, swapped))
    far = send(first, ON_Y, "r_far")
    swapped_late = tie(swapped_late)
    first, part_on, part_own = tie(
        *grad_blocks(NZ, 0, 3, factor, own, swapped, swapped_late)
    )
    near_back = send(first, BACK_Y, "r_back")

    mix = tie(mix_start(place, slope, islands, master, outer_params, outer_momentum))
    mix_x = send_island(mix.astype(BF16), SWAP_H, "frag_h")
    za = tie(za)
    zc = send(za, ON_Z, "z_far")
    zb = tie(zb)
    mix_x = tie(mix_x)
    mix = tie(mix + mix_x.astype(F32))
    mix_x = send_island(mix, PAIR_X, "frag_x1")
    far, near_back = tie(far, near_back)
    near_on = send(tie(*add(part_on, far)), ON_Y, "r_on")
    zc = tie(zc)
    near = tie(join([w_half, za, zb, zc]))
    z_order = (0, 1, 3, 2)
    swap_near = send(near, SWAP, "swap_near")
    ga = send(near, ON_Y, "g_on")
    gb = send(near, BACK_Y, "g_back")
    mix_x = tie(mix_x)
    mix = tie(mix + mix_x)
    mix_x = send_island(mix, CROSS_X, "frag_x2")
    mix_x = tie(mix_x)
    mix = tie(mix + mix_x)

    def batch(groups, back):
        pieces, places = [], []
        for piece, swapped, t in groups:
            pieces += [piece, swapped]
            places += [entry(core, t, s) for core in (0, 1) for s in z_order]
        return tie(input_blocks(table, places, cotan, pieces, width, factor, back))

    near_on = tie(near_on)
    z_far, z_back, z_on, z_own = tie(*add(part_own, near_back, near_on, split=True))
    far = send(z_far, ON_Z, "rz_far")
    near_back = send(z_back, BACK_Z, "rz_back")
    swap_near = tie(swap_near)
    back = batch([(near, swap_near, 0)], None)
    far = tie(far)
    near_on = send(tie(add_one(z_on, far)), ON_Z, "rz_on")
    ga = tie(ga)
    gc = send(ga, ON_Y, "g_far")
    swap_1 = send(ga, SWAP, "swap_on")
    gb = tie(gb)
    swap_3 = send(gb, SWAP, "swap_back")
    swap_1, swap_3 = tie(swap_1, swap_3)
    back = batch([(ga, swap_1, 1), (gb, swap_3, 3)], back)
    near_back, near_on = tie(near_back, near_on)
    gc = tie(gc)
    swap_2 = send(gc, SWAP, "swap_far")
    merged, moment_one, moment_two, outer_next, momentum_next = tie(
        *inner_step(
            place,
            slope,
            z_own,
            near_back,
            near_on,
            master,
            first_moment[0],
            second_moment[0],
            mix,
            outer_params,
            outer_momentum,
        )
    )
    swap_2 = tie(swap_2)
    back = batch([(gc, swap_2, 2)], back)
    return (
        back[None],
        merged[None],
        moment_one[None],
        moment_two[None],
        outer_next,
        momentum_next,
    )


def solution(mesh):
    return jax.shard_map(
        local,
        mesh=mesh,
        in_specs=(
            P("island", "fsdp", None),
            P("island", "fsdp", None),
            P("island", "fsdp", None),
            P("island", "fsdp", None),
            P("island", "fsdp", None),
            P(("fsdp", "island"), None),
            P(("fsdp", "island"), None),
            P(),
        ),
        out_specs=(
            P("island", "fsdp", None),
            P("island", "fsdp", None),
            P("island", "fsdp", None),
            P("island", "fsdp", None),
            P(("fsdp", "island"), None),
            P(("fsdp", "island"), None),
        ),
        check_vma=False,
    )
```

time: 257 us -> 106 us (0.41); the launches traced: 252 us -> 106 us
  waiting for transfers between devices: 132 us -> 47.9 us
  blocking collectives: 79.6 us -> 0 us
  starting transfers between devices: 0.12 us -> 33.5 us
  Pallas kernels: 0 us -> 17.2 us
  matrix products: 15.6 us -> 0 us
  between operations: 16.3 us -> 1.94 us
  other arithmetic: 5.05 us -> 0.13 us
    reduce_scatter x1 -> x0, waiting for transfers between devices: 132 us -> none  [local(): lax.psum_scatter((lax.dot_general(tokens_in, cotan, (((0,), (0,)), ((), (...]
    all_gather x2 -> x0, blocking collectives: 79.6 us -> none  [the longest x1 41.1 us: local(): lax.all_gather(outer_params, 'island', axis=0, tiled=True)]
    ppermute x0 -> x21, waiting for transfers between devices: none -> 47.9 us  [the longest x18 35.2 us: send(): return lax.ppermute(value, 'fsdp', pairs)]
    ppermute x0 -> x21, starting transfers between devices: none -> 33.5 us  [the longest x18 25.4 us: send(): return lax.ppermute(value, 'fsdp', pairs)]
    pallas_call x0 -> x13, Pallas kernels: none -> 17.2 us  [the longest x3 6.83 us: input_blocks(): pl.pallas_call(body, out_shape=jax.ShapeDtypeStruct((cotan.shape[0], widt...]
    dot_general x2 -> x0, matrix products: 15.6 us -> none  [the longest x1 7.83 us: local(): lax.dot_general(cotan, lax.all_gather(w_half, 'fsdp', axis=0, tiled=True)...]
    unnamed x14 -> x20, local copies, waits for them, and re-layouts: 0.32 us -> 5.43 us
    broadcast_in_dim x2 -> x0, other arithmetic: 3.24 us -> none  [the longest x1 2.28 us: local(): moment_two[None]]
  transfers between devices with their start and end apart: 3 -> 21, of which waited for: 1 -> 14; matrix products, arithmetic and copies ran while one was open for 7% -> 0% of each run, Pallas kernels for 0% -> 13%
where the time goes in v1:
time: 106 us
  waiting for transfers between devices  47.9 us (45%)
  starting transfers between devices  33.5 us (32%)
  Pallas kernels  17.2 us (16%)
  local copies, waits for them, and re-layouts  5.54 us (5%)
  between operations  1.94 us (2%)
    ppermute x18, waiting for transfers between devices, send(): return lax.ppermute(value, 'fsdp', pairs)  35.2 us
    ppermute x18, starting transfers between devices, send(): return lax.ppermute(value, 'fsdp', pairs)  25.4 us
    ppermute x3, waiting for transfers between devices, send_island(): return lax.ppermute(value, 'island', pairs)  12.6 us
    ppermute x3, starting transfers between devices, send_island(): return lax.ppermute(value, 'island', pairs)  8.07 us
    pallas_call x3, Pallas kernels, input_blocks(): pl.pallas_call(body, out_shape=jax.ShapeDtypeStruct((cotan.shape[0], widt...  6.83 us
    unnamed x20, local copies, waits for them, and re-layouts  5.43 us
    pallas_call x2, Pallas kernels, grad_blocks(): pl.pallas_call(body, out_shape=[jax.ShapeDtypeStruct((NZ, halves * width,...  4.31 us
    pallas_call x1, Pallas kernels, inner_step(): pl.pallas_call(body, out_shape=[jax.ShapeDtypeStruct(master.shape, F32)]...  2.14 us
  transfers between devices with their start and end apart: 21, of which 14 were waited for; matrix products, arithmetic and copies ran while one was open for 0% of the time, Pallas kernels for 13%

profile of v1, /device:TPU:1, one launch (start us, length us, event | category | flops | bytes accessed | tf_op | source)
XLA Modules:
  0.0 106.1 jit_solution(10374216603123645507)
XLA Ops:
  1.0 0.1 stack.137.table
  1.1 2.2 %copy-done.1 = bf16[1,256,8192]{2,1,0:T(8,128)(2,1)S(1)} copy-done((bf16[1,256,8192]{2,1,0:T(8,128)(2,1)S(1)}, bf16[1,256,8192]{2,1,0:T(8,128)(2,1)}, u32[]{:S(2)}) %copy-start.1) | copy-done | bytes 4194328
  3.3 0.9 copy-done.2
  4.2 1.2 %shard_map.127 = (bf16[6,256,256]{2,1,0:T(8,128)(2,1)S(1)}, bf16[12,256,256]{2,1,0:T(8,128)(2,1)S(1)}, bf16[18,256,256]{2,1,0:T(8,128)(2,1)S(1)}) custom-call(s32[32]{0:T(128)S(1)} %stack.137.table, bf16[256,8192]{1,0:T(8,128)(2,1)S(1)} %bitcast.45, bf16[256,512]{1,0:T(8,128)(2,1)S(1)} %bitcast.46), custom_call_target="tpu_custom_call" | custom-call | flops 1 | bytes 1 | tf_op jit(solution)/shard_map/pallas_call | solution.py:96
  5.4 3.3 %collective-permute-start.1 = (bf16[12,256,256]{2,1,0:T(8,128)(2,1)S(1)}, bf16[12,256,256]{2,1,0:T(8,128)(2,1)S(1)}, u32[]{:S(2)}, u32[]{:S(2)}) collective-permute-start(bf16[12,256,256]{2,1,0:T(8,128)(2,1)S(1)} %get-tuple-element.116), channel_id=1, source_target_pairs={{0,1},{1,0},{2,3},{3,2},{4,5},{5,4},{6,7},{7,6},{8,9},{9,8},{10,11... | collective-permute-start | bytes 4718600 | tf_op jit(solution)/shard_map/swap_inputs_late/ppermute | solution.py:306
  8.7 0.1 collective-permute-start
  8.9 4.0 %collective-permute-done.swapped.packed = bf16[6,256,256]{2,1,0:T(8,128)(2,1)S(1)} collective-permute-done((bf16[6,256,256]{2,1,0:T(8,128)(2,1)S(1)}, bf16[6,256,256]{2,1,0:T(8,128)(2,1)S(1)}, u32[]{:S(2)}, u32[]{:S(2)}) %collective-permute-start) | collective-permute-done | bytes 786464 | tf_op jit(solution)/shard_map/swap_inputs/ppermute | solution.py:306
  12.9 1.7 %shard_map.129 = bf16[4,512,256]{2,1,0:T(8,128)(2,1)} custom-call(bf16[18,256,256]{2,1,0:T(8,128)(2,1)S(1)} %get-tuple-element.113.own, bf16[6,256,256]{2,1,0:T(8,128)(2,1)S(1)} %collective-permute-done.swapped.packed, bf16[6,256,256]{2,1,0:T(8,128)(2,1)S(1)} %collective-permute-done.swapped.packed), custom_call_target="tpu_custom_call" | custom-call | flops 1 | bytes 1 | tf_op jit(solution)/shard_map/pallas_call | solution.py:142
  14.5 1.0 collective-permute-start.5
  15.5 2.6 %shard_map.130 = (bf16[4,512,256]{2,1,0:T(8,128)(2,1)}, bf16[4,512,256]{2,1,0:T(8,128)(2,1)S(1)}, bf16[4,512,256]{2,1,0:T(8,128)(2,1)S(1)}) custom-call(bf16[18,256,256]{2,1,0:T(8,128)(2,1)S(1)} %get-tuple-element.113.own, bf16[6,256,256]{2,1,0:T(8,128)(2,1)S(1)} %collective-permute-done.swapped.packed, bf16[12,256,256]{2,1,0:T(8,128)(2,1)S(1)} %collective-permute-done.1.packed), custom_call_target="tpu_custom_call" | custom-call | flops 1 | bytes 1 | tf_op jit(solution)/shard_map/pallas_call | solution.py:142
  18.2 1.0 copy-done.4
  19.2 0.5 collective-permute-start.6
  19.7 3.9 %collective-permute-start.2 = (bf16[256,512]{1,0:T(8,128)(2,1)S(1)}, bf16[256,512]{1,0:T(8,128)(2,1)S(1)}, u32[]{:S(2)}, u32[]{:S(2)}) collective-permute-start(bf16[256,512]{1,0:T(8,128)(2,1)S(1)} %shard_map.128.refs_0_), channel_id=1, source_target_pairs={{0,8},{1,25},{2,10},{3,27},{4,12},{5,29},{6,14},{7,31},{8,16},{9,1... | collective-permute-start | bytes 786440 | tf_op jit(solution)/shard_map/z_on/ppermute | solution.py:306
  24.2 0.1 pad_add_fusion.place
  24.3 0.7 shard_map.131
  25.0 4.3 %collective-permute-start.4 = (bf16[256,128]{1,0:T(8,128)(2,1)S(1)}, bf16[256,128]{1,0:T(8,128)(2,1)S(1)}, u32[]{:S(2)}, u32[]{:S(2)}) collective-permute-start(bf16[256,128]{1,0:T(8,128)(2,1)S(1)} %convert_element_type.6), channel_id=1, source_target_pairs={{0,128},{32,160},{64,192},{96,224},{128,0},{160,32},{192,64},{224,... | collective-permute-start | bytes 196616 | tf_op jit(solution)/shard_map/frag_h/ppermute | solution.py:310
  29.3 0.4 collective-permute-done.2.refs_1_
  29.8 4.7 %collective-permute-done.3.refs_2_ = bf16[256,512]{1,0:T(8,128)(2,1)S(1)} collective-permute-done((bf16[256,512]{1,0:T(8,128)(2,1)S(1)}, bf16[256,512]{1,0:T(8,128)(2,1)S(1)}, u32[]{:S(2)}, u32[]{:S(2)}) %collective-permute-start.3) | collective-permute-done | bytes 262176 | tf_op jit(solution)/shard_map/z_back/ppermute | solution.py:306
  34.5 1.3 %collective-permute-start.7 = (bf16[256,512]{1,0:T(8,128)(2,1)S(1)}, bf16[256,512]{1,0:T(8,128)(2,1)S(1)}, u32[]{:S(2)}, u32[]{:S(2)}) collective-permute-start(bf16[256,512]{1,0:T(8,128)(2,1)S(1)} %collective-permute-done.2.refs_1_), channel_id=1, source_target_pairs={{0,8},{1,25},{2,10},{3,27},{4,12},{5,29},{6,14},{7,31},{8,16},{9,1... | collective-permute-start | bytes 786440 | tf_op jit(solution)/shard_map/z_far/ppermute | solution.py:306
  35.8 6.9 %collective-permute-done.4 = bf16[256,128]{1,0:T(8,128)(2,1)S(1)} collective-permute-done((bf16[256,128]{1,0:T(8,128)(2,1)S(1)}, bf16[256,128]{1,0:T(8,128)(2,1)S(1)}, u32[]{:S(2)}, u32[]{:S(2)}) %collective-permute-start.4) | collective-permute-done | bytes 65568 | tf_op jit(solution)/shard_map/frag_h/ppermute | solution.py:310
  42.7 1.3 %copy-done.5 = bf16[4,512,256]{2,1,0:T(8,128)(2,1)S(1)} copy-done((bf16[4,512,256]{2,1,0:T(8,128)(2,1)S(1)}, bf16[4,512,256]{2,1,0:T(8,128)(2,1)}, u32[]{:S(2)}) %copy-start.5) | copy-done | bytes 1048600
  44.0 1.5 %shard_map.132 = bf16[4,512,256]{2,1,0:T(8,128)(2,1)S(1)} custom-call(bf16[4,512,256]{2,1,0:T(8,128)(2,1)S(1)} %copy-done.5, bf16[4,512,256]{2,1,0:T(8,128)(2,1)} %collective-permute-done.5.refs_1_), custom_call_target="tpu_custom_call" | custom-call | flops 1 | bytes 1 | tf_op jit(solution)/shard_map/pallas_call | solution.py:167
  45.4 2.1 %collective-permute-start.10 = (bf16[4,512,256]{2,1,0:T(8,128)(2,1)S(1)}, bf16[4,512,256]{2,1,0:T(8,128)(2,1)S(1)}, u32[]{:S(2)}, u32[]{:S(2)}) collective-permute-start(bf16[4,512,256]{2,1,0:T(8,128)(2,1)S(1)} %shard_map.132), channel_id=1, source_target_pairs={{0,2},{1,7},{2,4},{3,1},{4,6},{5,3},{6,0},{7,5},{8,10},{9,15},{10,... | collective-permute-start | bytes 3145736 | tf_op jit(solution)/shard_map/r_on/ppermute | solution.py:306
  47.5 0.1 shard_map.133.refs_0_
  47.6 0.1 collective-permute-start.11
  47.7 2.0 %collective-permute-start.13 = (bf16[1024,512]{1,0:T(8,128)(2,1)S(1)}, bf16[1024,512]{1,0:T(8,128)(2,1)S(1)}, u32[]{:S(2)}, u32[]{:S(2)}) collective-permute-start(bf16[1024,512]{1,0:T(8,128)(2,1)S(1)} %shard_map.133.refs_0_), channel_id=1, source_target_pairs={{0,2},{1,7},{2,4},{3,1},{4,6},{5,3},{6,0},{7,5},{8,10},{9,15},{10,... | collective-permute-start | bytes 3145736 | tf_op jit(solution)/shard_map/g_on/ppermute | solution.py:306
  49.8 1.2 %collective-permute-start.8 = (f32[256,128]{1,0:T(8,128)S(1)}, f32[256,128]{1,0:T(8,128)S(1)}, u32[]{:S(2)}, u32[]{:S(2)}) collective-permute-start(f32[256,128]{1,0:T(8,128)S(1)} %convert_add_fusion), channel_id=1, source_target_pairs={{0,32},{32,0},{64,96},{96,64},{128,160},{160,128},{192,224},{224,1... | collective-permute-start | bytes 393224 | tf_op jit(solution)/shard_map/frag_x1/ppermute | solution.py:310
  51.0 2.9 %collective-permute-done.8 = f32[256,128]{1,0:T(8,128)S(1)} collective-permute-done((f32[256,128]{1,0:T(8,128)S(1)}, f32[256,128]{1,0:T(8,128)S(1)}, u32[]{:S(2)}, u32[]{:S(2)}) %collective-permute-start.8) | collective-permute-done | bytes 131104 | tf_op jit(solution)/shard_map/frag_x1/ppermute | solution.py:310
  53.9 2.6 %collective-permute-start.9 = (f32[256,128]{1,0:T(8,128)S(1)}, f32[256,128]{1,0:T(8,128)S(1)}, u32[]{:S(2)}, u32[]{:S(2)}) collective-permute-start(f32[256,128]{1,0:T(8,128)S(1)} %add.487), channel_id=1, source_target_pairs={{0,96},{32,64},{64,32},{96,0},{128,224},{160,192},{192,160},{224,1... | collective-permute-start | bytes 393224 | tf_op jit(solution)/shard_map/frag_x2/ppermute | solution.py:310
  56.5 2.8 %collective-permute-done.9 = f32[256,128]{1,0:T(8,128)S(1)} collective-permute-done((f32[256,128]{1,0:T(8,128)S(1)}, f32[256,128]{1,0:T(8,128)S(1)}, u32[]{:S(2)}, u32[]{:S(2)}) %collective-permute-start.9) | collective-permute-done | bytes 131104 | tf_op jit(solution)/shard_map/frag_x2/ppermute | solution.py:310
  59.3 7.5 %collective-permute-done.10.refs_2_ = bf16[4,512,256]{2,1,0:T(8,128)(2,1)S(1)} collective-permute-done((bf16[4,512,256]{2,1,0:T(8,128)(2,1)S(1)}, bf16[4,512,256]{2,1,0:T(8,128)(2,1)S(1)}, u32[]{:S(2)}, u32[]{:S(2)}) %collective-permute-start.10) | collective-permute-done | bytes 1048608 | tf_op jit(solution)/shard_map/r_on/ppermute | solution.py:306
  66.9 0.4 shard_map.134
  67.3 1.8 %collective-permute-start.12 = (bf16[512,256]{1,0:T(8,128)(2,1)S(1)}, bf16[512,256]{1,0:T(8,128)(2,1)S(1)}, u32[]{:S(2)}, u32[]{:S(2)}) collective-permute-start(bf16[512,256]{1,0:T(8,128)(2,1)S(1)} %get-tuple-element.164), channel_id=1, source_target_pairs={{0,8},{1,25},{2,10},{3,27},{4,12},{5,29},{6,14},{7,31},{8,16},{9,1... | collective-permute-start | bytes 786440 | tf_op jit(solution)/shard_map/rz_far/ppermute | solution.py:306
  69.1 2.1 %shard_map.135.refs_4_ = bf16[256,8192]{1,0:T(8,128)(2,1)} custom-call(s32[32]{0:T(128)S(1)} %stack.137.table, bf16[256,512]{1,0:T(8,128)(2,1)S(1)} %bitcast.47, bf16[1024,512]{1,0:T(8,128)(2,1)S(1)} %shard_map.133.refs_0_, bf16[1024,512]{1,0:T(8,128)(2,1)S(1)} %collective-permute-done.11.refs_1_), custom_call_target="tpu_custom_call" | custom-call | flops 1 | bytes 1 | tf_op jit(solution)/shard_map/pallas_call | solution.py:220
  71.2 1.7 %collective-permute-done.12.b = bf16[512,256]{1,0:T(8,128)(2,1)S(1)} collective-permute-done((bf16[512,256]{1,0:T(8,128)(2,1)S(1)}, bf16[512,256]{1,0:T(8,128)(2,1)S(1)}, u32[]{:S(2)}, u32[]{:S(2)}) %collective-permute-start.12) | collective-permute-done | bytes 262176 | tf_op jit(solution)/shard_map/rz_far/ppermute | solution.py:306
  72.9 9.0 %collective-permute-done.13.refs_0_ = bf16[1024,512]{1,0:T(8,128)(2,1)S(1)} collective-permute-done((bf16[1024,512]{1,0:T(8,128)(2,1)S(1)}, bf16[1024,512]{1,0:T(8,128)(2,1)S(1)}, u32[]{:S(2)}, u32[]{:S(2)}) %collective-permute-start.13) | collective-permute-done | bytes 1048608 | tf_op jit(solution)/shard_map/g_on/ppermute | solution.py:306
  81.9 3.2 %collective-permute-start.16 = (bf16[1024,512]{1,0:T(8,128)(2,1)S(1)}, bf16[1024,512]{1,0:T(8,128)(2,1)S(1)}, u32[]{:S(2)}, u32[]{:S(2)}) collective-permute-start(bf16[1024,512]{1,0:T(8,128)(2,1)S(1)} %collective-permute-done.14.refs_2_), channel_id=1, source_target_pairs={{0,1},{1,0},{2,3},{3,2},{4,5},{5,4},{6,7},{7,6},{8,9},{9,8},{10,11... | collective-permute-start | bytes 3145736 | tf_op jit(solution)/shard_map/swap_back/ppermute | solution.py:306
  85.1 0.3 collective-permute-start.19
  85.4 3.3 %collective-permute-start.18 = (bf16[512,256]{1,0:T(8,128)(2,1)S(1)}, bf16[512,256]{1,0:T(8,128)(2,1)S(1)}, u32[]{:S(2)}, u32[]{:S(2)}) collective-permute-start(bf16[512,256]{1,0:T(8,128)(2,1)S(1)} %shard_map.136), channel_id=1, source_target_pairs={{0,8},{1,25},{2,10},{3,27},{4,12},{5,29},{6,14},{7,31},{8,16},{9,1... | collective-permute-start | bytes 786440 | tf_op jit(solution)/shard_map/rz_on/ppermute | solution.py:306
  88.7 0.3 collective-permute-done.15.refs_1_
  88.9 2.7 %shard_map.137.refs_2_ = bf16[256,8192]{1,0:T(8,128)(2,1)} custom-call(s32[32]{0:T(128)S(1)} %stack.137.table, bf16[256,512]{1,0:T(8,128)(2,1)S(1)} %bitcast.48, bf16[1024,512]{1,0:T(8,128)(2,1)S(1)} %collective-permute-done.13.refs_0_, bf16[1024,512]{1,0:T(8,128)(2,1)S(1)} %collective-permute-done.15.refs_1_, ...), custom_call_target="tpu_custom_call", output_to_operand_aliasing={{}: (6, {})} | custom-call | flops 1 | bytes 1 | tf_op jit(solution)/shard_map/pallas_call | solution.py:220
  91.6 3.9 %collective-permute-done.17.one = bf16[512,256]{1,0:T(8,128)(2,1)S(1)} collective-permute-done((bf16[512,256]{1,0:T(8,128)(2,1)S(1)}, bf16[512,256]{1,0:T(8,128)(2,1)S(1)}, u32[]{:S(2)}, u32[]{:S(2)}) %collective-permute-start.17) | collective-permute-done | bytes 262176 | tf_op jit(solution)/shard_map/rz_back/ppermute | solution.py:306
  95.6 2.7 %collective-permute-done.18.two = bf16[512,256]{1,0:T(8,128)(2,1)S(1)} collective-permute-done((bf16[512,256]{1,0:T(8,128)(2,1)S(1)}, bf16[512,256]{1,0:T(8,128)(2,1)S(1)}, u32[]{:S(2)}, u32[]{:S(2)}) %collective-permute-start.18) | collective-permute-done | bytes 262176 | tf_op jit(solution)/shard_map/rz_on/ppermute | solution.py:306
  98.3 0.8 collective-permute-done.19.refs_0_
  99.1 2.6 %collective-permute-start.20 = (bf16[1024,512]{1,0:T(8,128)(2,1)S(1)}, bf16[1024,512]{1,0:T(8,128)(2,1)S(1)}, u32[]{:S(2)}, u32[]{:S(2)}) collective-permute-start(bf16[1024,512]{1,0:T(8,128)(2,1)S(1)} %collective-permute-done.19.refs_0_), channel_id=1, source_target_pairs={{0,1},{1,0},{2,3},{3,2},{4,5},{5,4},{6,7},{7,6},{8,9},{9,8},{10,11... | collective-permute-start | bytes 3145736 | tf_op jit(solution)/shard_map/swap_far/ppermute | solution.py:306
  101.6 2.1 %shard_map.138 = (f32[256,512]{1,0:T(8,128)}, f32[256,512]{1,0:T(8,128)}, f32[256,512]{1,0:T(8,128)}, f32[32,128]{1,0:T(8,128)}, f32[32,128]{1,0:T(8,128)}) custom-call(s32[2]{0:T(128)S(1)} %pad_add_fusion.place, bf16[512,256]{1,0:T(8,128)(2,1)S(1)} %get-tuple-element.182.own, bf16[512,256]{1,0:T(8,128)(2,1)S(1)} %collective-permute-done.17.one, ...), custom_call_target="tpu_custom_call" | custom-call | flops 1 | bytes 1 | tf_op jit(solution)/shard_map/pallas_call | solution.py:283
  103.8 0.1 collective-permute-done.20.refs_1_
  103.9 2.1 %shard_map.139 = bf16[256,8192]{1,0:T(8,128)(2,1)} custom-call(s32[32]{0:T(128)S(1)} %stack.137.table, bf16[256,512]{1,0:T(8,128)(2,1)S(1)} %bitcast.49, bf16[1024,512]{1,0:T(8,128)(2,1)S(1)} %collective-permute-done.19.refs_0_, bf16[1024,512]{1,0:T(8,128)(2,1)S(1)} %collective-permute-done.20.refs_1_, ...), custom_call_target="tpu_custom_call", output_to_operand_aliasing={{}: (4, {})} | custom-call | flops 1 | bytes 1 | tf_op jit(solution)/shard_map/pallas_call | solution.py:220
  (33 shorter events, 0.2 us)
Async XLA Ops:
  0.6 8.2 %copy-start = (f32[1,256,512]{2,1,0:T(8,128)S(1)}, f32[1,256,512]{2,1,0:T(8,128)}, u32[]{:S(2)}) copy-start(f32[1,256,512]{2,1,0:T(8,128)} %param.10) | copy-start | bytes 1572868
  1.1 2.2 %copy-start.1 = (bf16[1,256,8192]{2,1,0:T(8,128)(2,1)S(1)}, bf16[1,256,8192]{2,1,0:T(8,128)(2,1)}, u32[]{:S(2)}) copy-start(bf16[1,256,8192]{2,1,0:T(8,128)(2,1)} %param.8) | copy-start | bytes 12582916
  3.3 0.9 copy-start.2
  5.4 10.2 %collective-permute-start.1 = (bf16[12,256,256]{2,1,0:T(8,128)(2,1)S(1)}, bf16[12,256,256]{2,1,0:T(8,128)(2,1)S(1)}, u32[]{:S(2)}, u32[]{:S(2)}) collective-permute-start(bf16[12,256,256]{2,1,0:T(8,128)(2,1)S(1)} %get-tuple-element.116), channel_id=1, source_target_pairs={{0,1},{1,0},{2,3},{3,2},{4,5},{5,4},{6,7},{7,6},{8,9},{9,8},{10,11... | collective-permute-start | bytes 4718600 | tf_op jit(solution)/shard_map/swap_inputs_late/ppermute | solution.py:306
  8.7 4.2 %collective-permute-start = (bf16[6,256,256]{2,1,0:T(8,128)(2,1)S(1)}, bf16[6,256,256]{2,1,0:T(8,128)(2,1)S(1)}, u32[]{:S(2)}, u32[]{:S(2)}) collective-permute-start(bf16[6,256,256]{2,1,0:T(8,128)(2,1)S(1)} %get-tuple-element.111), channel_id=1, source_target_pairs={{0,1},{1,0},{2,3},{3,2},{4,5},{5,4},{6,7},{7,6},{8,9},{9,8},{10,11... | collective-permute-start | bytes 2359304 | tf_op jit(solution)/shard_map/swap_inputs/ppermute | solution.py:306
  8.8 15.4 %copy-start.8 = (f32[32,128]{1,0:T(8,128)S(1)}, f32[32,128]{1,0:T(8,128)}, u32[]{:S(2)}) copy-start(f32[32,128]{1,0:T(8,128)} %outer.3) | copy-start | bytes 49156
  8.9 15.4 %copy-start.9 = (f32[32,128]{1,0:T(8,128)S(1)}, f32[32,128]{1,0:T(8,128)}, u32[]{:S(2)}) copy-start(f32[32,128]{1,0:T(8,128)} %momentum.3) | copy-start | bytes 49156
  14.5 28.2 %collective-permute-start.5 = (bf16[4,512,256]{2,1,0:T(8,128)(2,1)}, bf16[4,512,256]{2,1,0:T(8,128)(2,1)}, u32[]{:S(2)}, u32[]{:S(2)}) collective-permute-start(bf16[4,512,256]{2,1,0:T(8,128)(2,1)} %shard_map.129), channel_id=1, source_target_pairs={{0,2},{1,7},{2,4},{3,1},{4,6},{5,3},{6,0},{7,5},{8,10},{9,15},{10,... | collective-permute-start | bytes 3145736 | tf_op jit(solution)/shard_map/r_far/ppermute | solution.py:306
  18.2 1.0 copy-start.4
  19.2 23.5 %collective-permute-start.6 = (bf16[4,512,256]{2,1,0:T(8,128)(2,1)}, bf16[4,512,256]{2,1,0:T(8,128)(2,1)S(1)}, u32[]{:S(2)}, u32[]{:S(2)}) collective-permute-start(bf16[4,512,256]{2,1,0:T(8,128)(2,1)} %get-tuple-element.132), channel_id=1, source_target_pairs={{0,6},{1,3},{2,0},{3,5},{4,2},{5,7},{6,4},{7,1},{8,14},{9,11},{10,... | collective-permute-start | bytes 3145736 | tf_op jit(solution)/shard_map/r_back/ppermute | solution.py:306
  19.7 10.1 %collective-permute-start.2 = (bf16[256,512]{1,0:T(8,128)(2,1)S(1)}, bf16[256,512]{1,0:T(8,128)(2,1)S(1)}, u32[]{:S(2)}, u32[]{:S(2)}) collective-permute-start(bf16[256,512]{1,0:T(8,128)(2,1)S(1)} %shard_map.128.refs_0_), channel_id=1, source_target_pairs={{0,8},{1,25},{2,10},{3,27},{4,12},{5,29},{6,14},{7,31},{8,16},{9,1... | collective-permute-start | bytes 786440 | tf_op jit(solution)/shard_map/z_on/ppermute | solution.py:306
  23.5 10.9 %collective-permute-start.3 = (bf16[256,512]{1,0:T(8,128)(2,1)S(1)}, bf16[256,512]{1,0:T(8,128)(2,1)S(1)}, u32[]{:S(2)}, u32[]{:S(2)}) collective-permute-start(bf16[256,512]{1,0:T(8,128)(2,1)S(1)} %shard_map.128.refs_0_), channel_id=1, source_target_pairs={{0,24},{1,9},{2,26},{3,11},{4,28},{5,13},{6,30},{7,15},{8,0},{9,17... | collective-permute-start | bytes 786440 | tf_op jit(solution)/shard_map/z_back/ppermute | solution.py:306
  25.0 17.6 %collective-permute-start.4 = (bf16[256,128]{1,0:T(8,128)(2,1)S(1)}, bf16[256,128]{1,0:T(8,128)(2,1)S(1)}, u32[]{:S(2)}, u32[]{:S(2)}) collective-permute-start(bf16[256,128]{1,0:T(8,128)(2,1)S(1)} %convert_element_type.6), channel_id=1, source_target_pairs={{0,128},{32,160},{64,192},{96,224},{128,0},{160,32},{192,64},{224,... | collective-permute-start | bytes 196616 | tf_op jit(solution)/shard_map/frag_h/ppermute | solution.py:310
  34.5 13.1 %collective-permute-start.7 = (bf16[256,512]{1,0:T(8,128)(2,1)S(1)}, bf16[256,512]{1,0:T(8,128)(2,1)S(1)}, u32[]{:S(2)}, u32[]{:S(2)}) collective-permute-start(bf16[256,512]{1,0:T(8,128)(2,1)S(1)} %collective-permute-done.2.refs_1_), channel_id=1, source_target_pairs={{0,8},{1,25},{2,10},{3,27},{4,12},{5,29},{6,14},{7,31},{8,16},{9,1... | collective-permute-start | bytes 786440 | tf_op jit(solution)/shard_map/z_far/ppermute | solution.py:306
  42.7 26.4 %copy-start.3 = (bf16[1,256,512]{2,1,0:T(8,128)(2,1)S(1)}, bf16[1,256,512]{2,1,0:T(8,128)(2,1)}, u32[]{:S(2)}) copy-start(bf16[1,256,512]{2,1,0:T(8,128)(2,1)} %param.9) | copy-start | bytes 786436
  42.7 1.3 %copy-start.5 = (bf16[4,512,256]{2,1,0:T(8,128)(2,1)S(1)}, bf16[4,512,256]{2,1,0:T(8,128)(2,1)}, u32[]{:S(2)}) copy-start(bf16[4,512,256]{2,1,0:T(8,128)(2,1)} %copy-done.4) | copy-start | bytes 3145732
  45.4 21.4 %collective-permute-start.10 = (bf16[4,512,256]{2,1,0:T(8,128)(2,1)S(1)}, bf16[4,512,256]{2,1,0:T(8,128)(2,1)S(1)}, u32[]{:S(2)}, u32[]{:S(2)}) collective-permute-start(bf16[4,512,256]{2,1,0:T(8,128)(2,1)S(1)} %shard_map.132), channel_id=1, source_target_pairs={{0,2},{1,7},{2,4},{3,1},{4,6},{5,3},{6,0},{7,5},{8,10},{9,15},{10,... | collective-permute-start | bytes 3145736 | tf_op jit(solution)/shard_map/r_on/ppermute | solution.py:306
  47.6 21.5 %collective-permute-start.11 = (bf16[1024,512]{1,0:T(8,128)(2,1)S(1)}, bf16[1024,512]{1,0:T(8,128)(2,1)S(1)}, u32[]{:S(2)}, u32[]{:S(2)}) collective-permute-start(bf16[1024,512]{1,0:T(8,128)(2,1)S(1)} %shard_map.133.refs_0_), channel_id=1, source_target_pairs={{0,1},{1,0},{2,3},{3,2},{4,5},{5,4},{6,7},{7,6},{8,9},{9,8},{10,11... | collective-permute-start | bytes 3145736 | tf_op jit(solution)/shard_map/swap_near/ppermute | solution.py:306
  47.7 34.2 %collective-permute-start.13 = (bf16[1024,512]{1,0:T(8,128)(2,1)S(1)}, bf16[1024,512]{1,0:T(8,128)(2,1)S(1)}, u32[]{:S(2)}, u32[]{:S(2)}) collective-permute-start(bf16[1024,512]{1,0:T(8,128)(2,1)S(1)} %shard_map.133.refs_0_), channel_id=1, source_target_pairs={{0,2},{1,7},{2,4},{3,1},{4,6},{5,3},{6,0},{7,5},{8,10},{9,15},{10,... | collective-permute-start | bytes 3145736 | tf_op jit(solution)/shard_map/g_on/ppermute | solution.py:306
  49.8 32.2 %collective-permute-start.14 = (bf16[1024,512]{1,0:T(8,128)(2,1)S(1)}, bf16[1024,512]{1,0:T(8,128)(2,1)S(1)}, u32[]{:S(2)}, u32[]{:S(2)}) collective-permute-start(bf16[1024,512]{1,0:T(8,128)(2,1)S(1)} %shard_map.133.refs_0_), channel_id=1, source_target_pairs={{0,6},{1,3},{2,0},{3,5},{4,2},{5,7},{6,4},{7,1},{8,14},{9,11},{10,... | collective-permute-start | bytes 3145736 | tf_op jit(solution)/shard_map/g_back/ppermute | solution.py:306
  49.8 4.1 %collective-permute-start.8 = (f32[256,128]{1,0:T(8,128)S(1)}, f32[256,128]{1,0:T(8,128)S(1)}, u32[]{:S(2)}, u32[]{:S(2)}) collective-permute-start(f32[256,128]{1,0:T(8,128)S(1)} %convert_add_fusion), channel_id=1, source_target_pairs={{0,32},{32,0},{64,96},{96,64},{128,160},{160,128},{192,224},{224,1... | collective-permute-start | bytes 393224 | tf_op jit(solution)/shard_map/frag_x1/ppermute | solution.py:310
  53.9 5.4 %collective-permute-start.9 = (f32[256,128]{1,0:T(8,128)S(1)}, f32[256,128]{1,0:T(8,128)S(1)}, u32[]{:S(2)}, u32[]{:S(2)}) collective-permute-start(f32[256,128]{1,0:T(8,128)S(1)} %add.487), channel_id=1, source_target_pairs={{0,96},{32,64},{64,32},{96,0},{128,224},{160,192},{192,160},{224,1... | collective-permute-start | bytes 393224 | tf_op jit(solution)/shard_map/frag_x2/ppermute | solution.py:310
  67.3 5.6 %collective-permute-start.12 = (bf16[512,256]{1,0:T(8,128)(2,1)S(1)}, bf16[512,256]{1,0:T(8,128)(2,1)S(1)}, u32[]{:S(2)}, u32[]{:S(2)}) collective-permute-start(bf16[512,256]{1,0:T(8,128)(2,1)S(1)} %get-tuple-element.164), channel_id=1, source_target_pairs={{0,8},{1,25},{2,10},{3,27},{4,12},{5,29},{6,14},{7,31},{8,16},{9,1... | collective-permute-start | bytes 786440 | tf_op jit(solution)/shard_map/rz_far/ppermute | solution.py:306
  72.9 28.7 %copy-start.6 = (f32[1,256,512]{2,1,0:T(8,128)S(1)}, f32[1,256,512]{2,1,0:T(8,128)}, u32[]{:S(2)}) copy-start(f32[1,256,512]{2,1,0:T(8,128)} %param.11) | copy-start | bytes 1572868
  72.9 28.7 %copy-start.7 = (f32[1,256,512]{2,1,0:T(8,128)S(1)}, f32[1,256,512]{2,1,0:T(8,128)}, u32[]{:S(2)}) copy-start(f32[1,256,512]{2,1,0:T(8,128)} %param.12) | copy-start | bytes 1572868
  81.9 6.7 %collective-permute-start.16 = (bf16[1024,512]{1,0:T(8,128)(2,1)S(1)}, bf16[1024,512]{1,0:T(8,128)(2,1)S(1)}, u32[]{:S(2)}, u32[]{:S(2)}) collective-permute-start(bf16[1024,512]{1,0:T(8,128)(2,1)S(1)} %collective-permute-done.14.refs_2_), channel_id=1, source_target_pairs={{0,1},{1,0},{2,3},{3,2},{4,5},{5,4},{6,7},{7,6},{8,9},{9,8},{10,11... | collective-permute-start | bytes 3145736 | tf_op jit(solution)/shard_map/swap_back/ppermute | solution.py:306
  85.1 3.8 %collective-permute-start.15 = (bf16[1024,512]{1,0:T(8,128)(2,1)S(1)}, bf16[1024,512]{1,0:T(8,128)(2,1)S(1)}, u32[]{:S(2)}, u32[]{:S(2)}) collective-permute-start(bf16[1024,512]{1,0:T(8,128)(2,1)S(1)} %collective-permute-done.13.refs_0_), channel_id=1, source_target_pairs={{0,1},{1,0},{2,3},{3,2},{4,5},{5,4},{6,7},{7,6},{8,9},{9,8},{10,11... | collective-permute-start | bytes 3145736 | tf_op jit(solution)/shard_map/swap_on/ppermute | solution.py:306
  85.1 13.9 %collective-permute-start.19 = (bf16[1024,512]{1,0:T(8,128)(2,1)S(1)}, bf16[1024,512]{1,0:T(8,128)(2,1)S(1)}, u32[]{:S(2)}, u32[]{:S(2)}) collective-permute-start(bf16[1024,512]{1,0:T(8,128)(2,1)S(1)} %collective-permute-done.13.refs_0_), channel_id=1, source_target_pairs={{0,2},{1,7},{2,4},{3,1},{4,6},{5,3},{6,0},{7,5},{8,10},{9,15},{10,... | collective-permute-start | bytes 3145736 | tf_op jit(solution)/shard_map/g_far/ppermute | solution.py:306
  85.4 10.2 %collective-permute-start.17 = (bf16[512,256]{1,0:T(8,128)(2,1)S(1)}, bf16[512,256]{1,0:T(8,128)(2,1)S(1)}, u32[]{:S(2)}, u32[]{:S(2)}) collective-permute-start(bf16[512,256]{1,0:T(8,128)(2,1)S(1)} %get-tuple-element.178), channel_id=1, source_target_pairs={{0,24},{1,9},{2,26},{3,11},{4,28},{5,13},{6,30},{7,15},{8,0},{9,17... | collective-permute-start | bytes 786440 | tf_op jit(solution)/shard_map/rz_back/ppermute | solution.py:306
  85.4 12.9 %collective-permute-start.18 = (bf16[512,256]{1,0:T(8,128)(2,1)S(1)}, bf16[512,256]{1,0:T(8,128)(2,1)S(1)}, u32[]{:S(2)}, u32[]{:S(2)}) collective-permute-start(bf16[512,256]{1,0:T(8,128)(2,1)S(1)} %shard_map.136), channel_id=1, source_target_pairs={{0,8},{1,25},{2,10},{3,27},{4,12},{5,29},{6,14},{7,31},{8,16},{9,1... | collective-permute-start | bytes 786440 | tf_op jit(solution)/shard_map/rz_on/ppermute | solution.py:306
  99.1 4.9 %collective-permute-start.20 = (bf16[1024,512]{1,0:T(8,128)(2,1)S(1)}, bf16[1024,512]{1,0:T(8,128)(2,1)S(1)}, u32[]{:S(2)}, u32[]{:S(2)}) collective-permute-start(bf16[1024,512]{1,0:T(8,128)(2,1)S(1)} %collective-permute-done.19.refs_0_), channel_id=1, source_target_pairs={{0,1},{1,0},{2,3},{3,2},{4,5},{5,4},{6,7},{7,6},{8,9},{9,8},{10,11... | collective-permute-start | bytes 3145736 | tf_op jit(solution)/shard_map/swap_far/ppermute | solution.py:306

commit v2 on v1

--- a/solution.py
+++ b/solution.py
@@ -350,30 +350,20 @@
             rows,
         )
     )
-    swapped = send(swapping, SWAP, "swap_inputs")
-    swapped_late = send(swapping_late, SWAP, "swap_inputs_late")
+    swapped = tie(send(swapping, SWAP, "swap_inputs"))
+    swapped_late = send(tie(swapping_late), SWAP, "swap_inputs_late")
+    first = tie(*grad_blocks(0, 0, 1, factor, own, swapped, swapped))
+    far = send(first, ON_Y, "r_far")
+    swapped_late = tie(swapped_late)
+    first, part_on, part_own = tie(*grad_blocks(NZ, 0, 3, factor, own, swapped, swapped_late))
+    near_back = send(first, BACK_Y, "r_back")
     w_half = tie(halve(tie(master)))
     za = send(w_half, ON_Z, "z_on")
     zb = send(w_half, BACK_Z, "z_back")
-
-    swapped = tie(swapped)
-    first = tie(*grad_blocks(0, 0, 1, factor, own, swapped, swapped))
-    far = send(first, ON_Y, "r_far")
-    swapped_late = tie(swapped_late)
-    first, part_on, part_own = tie(
-        *grad_blocks(NZ, 0, 3, factor, own, swapped, swapped_late)
-    )
-    near_back = send(first, BACK_Y, "r_back")
-
-    mix = tie(mix_start(place, slope, islands, master, outer_params, outer_momentum))
-    mix_x = send_island(mix.astype(BF16), SWAP_H, "frag_h")
     za = tie(za)
     zc = send(za, ON_Z, "z_far")
     zb = tie(zb)
-    mix_x = tie(mix_x)
-    mix = tie(mix + mix_x.astype(F32))
-    mix_x = send_island(mix, PAIR_X, "frag_x1")
-    far, near_back = tie(far, near_back)
+    far = tie(far)
     near_on = send(tie(*add(part_on, far)), ON_Y, "r_on")
     zc = tie(zc)
     near = tie(join([w_half, za, zb, zc]))
@@ -381,11 +371,17 @@
     swap_near = send(near, SWAP, "swap_near")
     ga = send(near, ON_Y, "g_on")
     gb = send(near, BACK_Y, "g_back")
+    near_back = tie(near_back)
+    part_own = tie(*add(part_own, near_back))
+
+    mix = tie(mix_start(place, slope, islands, tie(master), outer_params, outer_momentum))
+    mix_x = send_island(mix.astype(BF16), SWAP_H, "frag_h")
+    mix_x = tie(mix_x)
+    mix = tie(mix + mix_x.astype(F32))
+    mix_x = send_island(mix, PAIR_X, "frag_x1")
     mix_x = tie(mix_x)
     mix = tie(mix + mix_x)
     mix_x = send_island(mix, CROSS_X, "frag_x2")
-    mix_x = tie(mix_x)
-    mix = tie(mix + mix_x)
 
     def batch(groups, back):
         pieces, places = [], []
@@ -395,20 +391,21 @@
         return tie(input_blocks(table, places, cotan, pieces, width, factor, back))
 
     near_on = tie(near_on)
-    z_far, z_back, z_on, z_own = tie(*add(part_own, near_back, near_on, split=True))
+    z_far, z_back, z_on, z_own = tie(*add(part_own, near_on, split=True))
     far = send(z_far, ON_Z, "rz_far")
+    swap_near = tie(swap_near)
     near_back = send(z_back, BACK_Z, "rz_back")
-    swap_near = tie(swap_near)
-    back = batch([(near, swap_near, 0)], None)
+    mix_x = tie(mix_x)
+    mix = tie(mix + mix_x)
     far = tie(far)
     near_on = send(tie(add_one(z_on, far)), ON_Z, "rz_on")
-    ga = tie(ga)
+    ga, gb = tie(ga, gb)
     gc = send(ga, ON_Y, "g_far")
     swap_1 = send(ga, SWAP, "swap_on")
-    gb = tie(gb)
     swap_3 = send(gb, SWAP, "swap_back")
     swap_1, swap_3 = tie(swap_1, swap_3)
-    back = batch([(ga, swap_1, 1), (gb, swap_3, 3)], back)
+    back = batch([(ga, swap_1, 1), (gb, swap_3, 3)], None)
+    back = batch([(near, swap_near, 0)], back)
     near_back, near_on = tie(near_back, near_on)
     gc = tie(gc)
     swap_2 = send(gc, SWAP, "swap_far")

time: 106 us -> 96 us (0.906)
  waiting for transfers between devices: 47.9 us -> 36.2 us
  Pallas kernels: 17.2 us -> 20 us
    ppermute x18, waiting for transfers between devices: 35.2 us -> 27.1 us  [send(): return lax.ppermute(value, 'fsdp', pairs)]
    ppermute x3, waiting for transfers between devices: 12.6 us -> 9.04 us  [send_island(): return lax.ppermute(value, 'island', pairs)]
    pallas_call x2 -> x3, Pallas kernels: 1.84 us -> 4.15 us  [add(): pl.pallas_call(body, out_shape=[jax.ShapeDtypeStruct(tuple(shape), BF16)...]
    ppermute x18, starting transfers between devices: 25.4 us -> 23.9 us  [send(): return lax.ppermute(value, 'fsdp', pairs)]
    pallas_call x3, Pallas kernels: 6.83 us -> 8.33 us  [input_blocks(): pl.pallas_call(body, out_shape=jax.ShapeDtypeStruct((cotan.shape[0], widt...]
  transfers between devices with their start and end apart: 21 -> 21, of which waited for: 14 -> 13; matrix products, arithmetic and copies ran while one was open for 0% -> 0% of each run, Pallas kernels for 13% -> 18%
where the time goes in v2:
time: 96 us; the launch traced here: 95.6 us
  waiting for transfers between devices  36.2 us (38%)
  starting transfers between devices  32.8 us (34%)
  Pallas kernels  20 us (21%)
  local copies, waits for them, and re-layouts  4.52 us (5%)
  between operations  1.98 us (2%)
    ppermute x18, waiting for transfers between devices, send(): return lax.ppermute(value, 'fsdp', pairs)  27.1 us
    ppermute x18, starting transfers between devices, send(): return lax.ppermute(value, 'fsdp', pairs)  23.9 us
    ppermute x3, waiting for transfers between devices, send_island(): return lax.ppermute(value, 'island', pairs)  9.04 us
    ppermute x3, starting transfers between devices, send_island(): return lax.ppermute(value, 'island', pairs)  8.92 us
    pallas_call x3, Pallas kernels, input_blocks(): pl.pallas_call(body, out_shape=jax.ShapeDtypeStruct((cotan.shape[0], widt...  8.33 us
    unnamed x20, local copies, waits for them, and re-layouts  4.4 us
    pallas_call x3, Pallas kernels, add(): pl.pallas_call(body, out_shape=[jax.ShapeDtypeStruct(tuple(shape), BF16)...  4.15 us
    pallas_call x2, Pallas kernels, grad_blocks(): pl.pallas_call(body, out_shape=[jax.ShapeDtypeStruct((NZ, halves * width,...  3.34 us
  transfers between devices with their start and end apart: 21, of which 13 were waited for; matrix products, arithmetic and copies ran while one was open for 0% of the time, Pallas kernels for 18%

profile of v2, /device:TPU:1, one launch (start us, length us, event | category | flops | bytes accessed | tf_op | source)
XLA Modules:
  0.0 95.6 jit_solution(9678898680514574170)
XLA Ops:
  0.9 0.1 stack.137.table
  1.1 0.9 copy-done.1
  2.0 2.2 %copy-done.3 = bf16[1,256,8192]{2,1,0:T(8,128)(2,1)S(1)} copy-done((bf16[1,256,8192]{2,1,0:T(8,128)(2,1)S(1)}, bf16[1,256,8192]{2,1,0:T(8,128)(2,1)}, u32[]{:S(2)}) %copy-start.3) | copy-done | bytes 4194328
  4.2 1.2 %shard_map.127 = (bf16[6,256,256]{2,1,0:T(8,128)(2,1)S(1)}, bf16[12,256,256]{2,1,0:T(8,128)(2,1)S(1)}, bf16[18,256,256]{2,1,0:T(8,128)(2,1)S(1)}) custom-call(s32[32]{0:T(128)S(1)} %stack.137.table, bf16[256,8192]{1,0:T(8,128)(2,1)S(1)} %bitcast.49, bf16[256,512]{1,0:T(8,128)(2,1)S(1)} %bitcast.45), custom_call_target="tpu_custom_call" | custom-call | flops 1 | bytes 1 | tf_op jit(solution)/shard_map/pallas_call | solution.py:96
  5.4 3.3 %collective-permute-start = (bf16[6,256,256]{2,1,0:T(8,128)(2,1)S(1)}, bf16[6,256,256]{2,1,0:T(8,128)(2,1)S(1)}, u32[]{:S(2)}, u32[]{:S(2)}) collective-permute-start(bf16[6,256,256]{2,1,0:T(8,128)(2,1)S(1)} %get-tuple-element.114), channel_id=1, source_target_pairs={{0,1},{1,0},{2,3},{3,2},{4,5},{5,4},{6,7},{7,6},{8,9},{9,8},{10,11... | collective-permute-start | bytes 2359304 | tf_op jit(solution)/shard_map/swap_inputs/ppermute | solution.py:306
  8.7 1.9 %collective-permute-done.swapped.packed = bf16[6,256,256]{2,1,0:T(8,128)(2,1)S(1)} collective-permute-done((bf16[6,256,256]{2,1,0:T(8,128)(2,1)S(1)}, bf16[6,256,256]{2,1,0:T(8,128)(2,1)S(1)}, u32[]{:S(2)}, u32[]{:S(2)}) %collective-permute-start) | collective-permute-done | bytes 786464 | tf_op jit(solution)/shard_map/swap_inputs/ppermute | solution.py:306
  10.6 0.4 collective-permute-start.1
  11.0 0.7 shard_map.128
  11.7 1.1 %collective-permute-start.4 = (bf16[4,512,256]{2,1,0:T(8,128)(2,1)S(1)}, bf16[4,512,256]{2,1,0:T(8,128)(2,1)S(1)}, u32[]{:S(2)}, u32[]{:S(2)}) collective-permute-start(bf16[4,512,256]{2,1,0:T(8,128)(2,1)S(1)} %shard_map.128), channel_id=1, source_target_pairs={{0,2},{1,7},{2,4},{3,1},{4,6},{5,3},{6,0},{7,5},{8,10},{9,15},{10,... | collective-permute-start | bytes 3145736 | tf_op jit(solution)/shard_map/r_far/ppermute | solution.py:306
  12.8 1.2 %collective-permute-done.1.packed = bf16[12,256,256]{2,1,0:T(8,128)(2,1)S(1)} collective-permute-done((bf16[12,256,256]{2,1,0:T(8,128)(2,1)S(1)}, bf16[12,256,256]{2,1,0:T(8,128)(2,1)S(1)}, u32[]{:S(2)}, u32[]{:S(2)}) %collective-permute-start.1) | collective-permute-done | bytes 1572896 | tf_op jit(solution)/shard_map/swap_inputs_late/ppermute | solution.py:306
  14.0 2.6 %shard_map.129 = (bf16[4,512,256]{2,1,0:T(8,128)(2,1)}, bf16[4,512,256]{2,1,0:T(8,128)(2,1)S(1)}, bf16[4,512,256]{2,1,0:T(8,128)(2,1)S(1)}) custom-call(bf16[18,256,256]{2,1,0:T(8,128)(2,1)S(1)} %get-tuple-element.118.own, bf16[6,256,256]{2,1,0:T(8,128)(2,1)S(1)} %collective-permute-done.swapped.packed, bf16[12,256,256]{2,1,0:T(8,128)(2,1)S(1)} %collective-permute-done.1.packed), custom_call_target="tpu_custom_call" | custom-call | flops 1 | bytes 1 | tf_op jit(solution)/shard_map/pallas_call | solution.py:142
  16.7 4.0 %collective-permute-start.2 = (bf16[256,512]{1,0:T(8,128)(2,1)S(1)}, bf16[256,512]{1,0:T(8,128)(2,1)S(1)}, u32[]{:S(2)}, u32[]{:S(2)}) collective-permute-start(bf16[256,512]{1,0:T(8,128)(2,1)S(1)} %shard_map.130.refs_0_), channel_id=1, source_target_pairs={{0,8},{1,25},{2,10},{3,27},{4,12},{5,29},{6,14},{7,31},{8,16},{9,1... | collective-permute-start | bytes 786440 | tf_op jit(solution)/shard_map/z_on/ppermute | solution.py:306
  20.7 6.1 %collective-permute-done.2.refs_1_ = bf16[256,512]{1,0:T(8,128)(2,1)S(1)} collective-permute-done((bf16[256,512]{1,0:T(8,128)(2,1)S(1)}, bf16[256,512]{1,0:T(8,128)(2,1)S(1)}, u32[]{:S(2)}, u32[]{:S(2)}) %collective-permute-start.2) | collective-permute-done | bytes 262176 | tf_op jit(solution)/shard_map/z_on/ppermute | solution.py:306
  26.8 5.5 %collective-permute-done.3.refs_2_ = bf16[256,512]{1,0:T(8,128)(2,1)S(1)} collective-permute-done((bf16[256,512]{1,0:T(8,128)(2,1)S(1)}, bf16[256,512]{1,0:T(8,128)(2,1)S(1)}, u32[]{:S(2)}, u32[]{:S(2)}) %collective-permute-start.3) | collective-permute-done | bytes 262176 | tf_op jit(solution)/shard_map/z_back/ppermute | solution.py:306
  32.4 1.2 %shard_map.131 = bf16[4,512,256]{2,1,0:T(8,128)(2,1)} custom-call(bf16[4,512,256]{2,1,0:T(8,128)(2,1)S(1)} %get-tuple-element.136.refs_0_, bf16[4,512,256]{2,1,0:T(8,128)(2,1)S(1)} %collective-permute-done.4.refs_1_), custom_call_target="tpu_custom_call" | custom-call | flops 1 | bytes 1 | tf_op jit(solution)/shard_map/pallas_call | solution.py:167
  33.6 3.3 %collective-permute-start.9 = (bf16[4,512,256]{2,1,0:T(8,128)(2,1)}, bf16[4,512,256]{2,1,0:T(8,128)(2,1)}, u32[]{:S(2)}, u32[]{:S(2)}) collective-permute-start(bf16[4,512,256]{2,1,0:T(8,128)(2,1)} %shard_map.131), channel_id=1, source_target_pairs={{0,2},{1,7},{2,4},{3,1},{4,6},{5,3},{6,0},{7,5},{8,10},{9,15},{10,... | collective-permute-start | bytes 3145736 | tf_op jit(solution)/shard_map/r_on/ppermute | solution.py:306
  36.9 4.7 %collective-permute-done.5.refs_3_ = bf16[256,512]{1,0:T(8,128)(2,1)S(1)} collective-permute-done((bf16[256,512]{1,0:T(8,128)(2,1)S(1)}, bf16[256,512]{1,0:T(8,128)(2,1)S(1)}, u32[]{:S(2)}, u32[]{:S(2)}) %collective-permute-start.5) | collective-permute-done | bytes 262176 | tf_op jit(solution)/shard_map/z_far/ppermute | solution.py:306
  41.6 0.1 shard_map.132.refs_0_
  41.7 0.1 collective-permute-start.10
  41.8 1.7 %collective-permute-start.14 = (bf16[1024,512]{1,0:T(8,128)(2,1)S(1)}, bf16[1024,512]{1,0:T(8,128)(2,1)}, u32[]{:S(2)}, u32[]{:S(2)}) collective-permute-start(bf16[1024,512]{1,0:T(8,128)(2,1)S(1)} %shard_map.132.refs_0_), channel_id=1, source_target_pairs={{0,6},{1,3},{2,0},{3,5},{4,2},{5,7},{6,4},{7,1},{8,14},{9,11},{10,... | collective-permute-start | bytes 3145736 | tf_op jit(solution)/shard_map/g_back/ppermute | solution.py:306
  43.5 1.0 %collective-permute-start.13 = (bf16[1024,512]{1,0:T(8,128)(2,1)S(1)}, bf16[1024,512]{1,0:T(8,128)(2,1)S(1)}, u32[]{:S(2)}, u32[]{:S(2)}) collective-permute-start(bf16[1024,512]{1,0:T(8,128)(2,1)S(1)} %shard_map.132.refs_0_), channel_id=1, source_target_pairs={{0,2},{1,7},{2,4},{3,1},{4,6},{5,3},{6,0},{7,5},{8,10},{9,15},{10,... | collective-permute-start | bytes 3145736 | tf_op jit(solution)/shard_map/g_on/ppermute | solution.py:306
  45.2 0.1 pad_add_fusion.place
  45.3 1.2 %copy-done.5 = bf16[4,512,256]{2,1,0:T(8,128)(2,1)S(1)} copy-done((bf16[4,512,256]{2,1,0:T(8,128)(2,1)S(1)}, bf16[4,512,256]{2,1,0:T(8,128)(2,1)}, u32[]{:S(2)}) %copy-start.5) | copy-done | bytes 1048600
  46.5 1.5 %shard_map.133.refs_0_ = bf16[4,512,256]{2,1,0:T(8,128)(2,1)S(1)} custom-call(bf16[4,512,256]{2,1,0:T(8,128)(2,1)S(1)} %copy-done.5, bf16[4,512,256]{2,1,0:T(8,128)(2,1)} %collective-permute-done.6.refs_1_), custom_call_target="tpu_custom_call" | custom-call | flops 1 | bytes 1 | tf_op jit(solution)/shard_map/pallas_call | solution.py:167
  48.0 0.7 shard_map.134
  48.7 5.0 %collective-permute-start.7 = (bf16[256,128]{1,0:T(8,128)(2,1)S(1)}, bf16[256,128]{1,0:T(8,128)(2,1)S(1)}, u32[]{:S(2)}, u32[]{:S(2)}) collective-permute-start(bf16[256,128]{1,0:T(8,128)(2,1)S(1)} %convert_element_type.6), channel_id=1, source_target_pairs={{0,128},{32,160},{64,192},{96,224},{128,0},{160,32},{192,64},{224,... | collective-permute-start | bytes 196616 | tf_op jit(solution)/shard_map/frag_h/ppermute | solution.py:310
  53.7 2.9 %collective-permute-done.7 = bf16[256,128]{1,0:T(8,128)(2,1)S(1)} collective-permute-done((bf16[256,128]{1,0:T(8,128)(2,1)S(1)}, bf16[256,128]{1,0:T(8,128)(2,1)S(1)}, u32[]{:S(2)}, u32[]{:S(2)}) %collective-permute-start.7) | collective-permute-done | bytes 65568 | tf_op jit(solution)/shard_map/frag_h/ppermute | solution.py:310
  56.6 1.5 %collective-permute-start.8 = (f32[256,128]{1,0:T(8,128)S(1)}, f32[256,128]{1,0:T(8,128)S(1)}, u32[]{:S(2)}, u32[]{:S(2)}) collective-permute-start(f32[256,128]{1,0:T(8,128)S(1)} %convert_add_fusion), channel_id=1, source_target_pairs={{0,32},{32,0},{64,96},{96,64},{128,160},{160,128},{192,224},{224,1... | collective-permute-start | bytes 393224 | tf_op jit(solution)/shard_map/frag_x1/ppermute | solution.py:310
  58.1 3.3 %collective-permute-done.8 = f32[256,128]{1,0:T(8,128)S(1)} collective-permute-done((f32[256,128]{1,0:T(8,128)S(1)}, f32[256,128]{1,0:T(8,128)S(1)}, u32[]{:S(2)}, u32[]{:S(2)}) %collective-permute-start.8) | collective-permute-done | bytes 131104 | tf_op jit(solution)/shard_map/frag_x1/ppermute | solution.py:310
  61.4 1.5 %shard_map.135 = (bf16[512,256]{1,0:T(8,128)(2,1)S(1)}, bf16[512,256]{1,0:T(8,128)(2,1)S(1)}, bf16[512,256]{1,0:T(8,128)(2,1)S(1)}, bf16[512,256]{1,0:T(8,128)(2,1)S(1)}) custom-call(bf16[4,512,256]{2,1,0:T(8,128)(2,1)S(1)} %shard_map.133.refs_0_, bf16[4,512,256]{2,1,0:T(8,128)(2,1)} %collective-permute-done.9.refs_1_), custom_call_target="tpu_custom_call" | custom-call | flops 1 | bytes 1 | tf_op jit(solution)/shard_map/pallas_call | solution.py:167
  62.9 1.0 %collective-permute-start.12 = (bf16[512,256]{1,0:T(8,128)(2,1)S(1)}, bf16[512,256]{1,0:T(8,128)(2,1)S(1)}, u32[]{:S(2)}, u32[]{:S(2)}) collective-permute-start(bf16[512,256]{1,0:T(8,128)(2,1)S(1)} %get-tuple-element.175), channel_id=1, source_target_pairs={{0,8},{1,25},{2,10},{3,27},{4,12},{5,29},{6,14},{7,31},{8,16},{9,1... | collective-permute-start | bytes 786440 | tf_op jit(solution)/shard_map/rz_far/ppermute | solution.py:306
  63.9 2.5 %collective-permute-start.11 = (f32[256,128]{1,0:T(8,128)S(1)}, f32[256,128]{1,0:T(8,128)S(1)}, u32[]{:S(2)}, u32[]{:S(2)}) collective-permute-start(f32[256,128]{1,0:T(8,128)S(1)} %add.487), channel_id=1, source_target_pairs={{0,96},{32,64},{64,32},{96,0},{128,224},{160,192},{192,160},{224,1... | collective-permute-start | bytes 393224 | tf_op jit(solution)/shard_map/frag_x2/ppermute | solution.py:310
  66.4 2.8 %collective-permute-done.11 = f32[256,128]{1,0:T(8,128)S(1)} collective-permute-done((f32[256,128]{1,0:T(8,128)S(1)}, f32[256,128]{1,0:T(8,128)S(1)}, u32[]{:S(2)}, u32[]{:S(2)}) %collective-permute-start.11) | collective-permute-done | bytes 131104 | tf_op jit(solution)/shard_map/frag_x2/ppermute | solution.py:310
  69.2 3.5 %collective-permute-done.12.b = bf16[512,256]{1,0:T(8,128)(2,1)S(1)} collective-permute-done((bf16[512,256]{1,0:T(8,128)(2,1)S(1)}, bf16[512,256]{1,0:T(8,128)(2,1)S(1)}, u32[]{:S(2)}, u32[]{:S(2)}) %collective-permute-start.12) | collective-permute-done | bytes 262176 | tf_op jit(solution)/shard_map/rz_far/ppermute | solution.py:306
  72.7 0.1 shard_map.136
  72.8 1.7 %collective-permute-start.16 = (bf16[1024,512]{1,0:T(8,128)(2,1)}, bf16[1024,512]{1,0:T(8,128)(2,1)S(1)}, u32[]{:S(2)}, u32[]{:S(2)}) collective-permute-start(bf16[1024,512]{1,0:T(8,128)(2,1)} %collective-permute-done.14.refs_2_), channel_id=1, source_target_pairs={{0,1},{1,0},{2,3},{3,2},{4,5},{5,4},{6,7},{7,6},{8,9},{9,8},{10,11... | collective-permute-start | bytes 3145736 | tf_op jit(solution)/shard_map/swap_back/ppermute | solution.py:306
  74.5 0.4 collective-permute-start.19
  74.9 0.6 collective-permute-start.17
  75.5 2.7 %collective-permute-start.18 = (bf16[512,256]{1,0:T(8,128)(2,1)S(1)}, bf16[512,256]{1,0:T(8,128)(2,1)S(1)}, u32[]{:S(2)}, u32[]{:S(2)}) collective-permute-start(bf16[512,256]{1,0:T(8,128)(2,1)S(1)} %shard_map.136), channel_id=1, source_target_pairs={{0,8},{1,25},{2,10},{3,27},{4,12},{5,29},{6,14},{7,31},{8,16},{9,1... | collective-permute-start | bytes 786440 | tf_op jit(solution)/shard_map/rz_on/ppermute | solution.py:306
  78.2 0.3 collective-permute-done.16.refs_3_
  78.5 3.4 %shard_map.137.refs_2_ = bf16[256,8192]{1,0:T(8,128)(2,1)} custom-call(s32[32]{0:T(128)S(1)} %stack.137.table, bf16[256,512]{1,0:T(8,128)(2,1)S(1)} %bitcast.46, bf16[1024,512]{1,0:T(8,128)(2,1)S(1)} %collective-permute-done.13.refs_0_, bf16[1024,512]{1,0:T(8,128)(2,1)S(1)} %collective-permute-done.15.refs_1_, ...), custom_call_target="tpu_custom_call" | custom-call | flops 1 | bytes 1 | tf_op jit(solution)/shard_map/pallas_call | solution.py:220
  81.9 2.8 %shard_map.138.refs_2_ = bf16[256,8192]{1,0:T(8,128)(2,1)} custom-call(s32[32]{0:T(128)S(1)} %stack.137.table, bf16[256,512]{1,0:T(8,128)(2,1)S(1)} %bitcast.47, bf16[1024,512]{1,0:T(8,128)(2,1)S(1)} %shard_map.132.refs_0_, bf16[1024,512]{1,0:T(8,128)(2,1)} %collective-permute-done.10.refs_1_, ...), custom_call_target="tpu_custom_call", output_to_operand_aliasing={{}: (4, {})} | custom-call | flops 1 | bytes 1 | tf_op jit(solution)/shard_map/pallas_call | solution.py:220
  84.8 2.4 %collective-permute-done.18.two = bf16[512,256]{1,0:T(8,128)(2,1)S(1)} collective-permute-done((bf16[512,256]{1,0:T(8,128)(2,1)S(1)}, bf16[512,256]{1,0:T(8,128)(2,1)S(1)}, u32[]{:S(2)}, u32[]{:S(2)}) %collective-permute-start.18) | collective-permute-done | bytes 262176 | tf_op jit(solution)/shard_map/rz_on/ppermute | solution.py:306
  87.2 1.3 %collective-permute-done.19.refs_0_ = bf16[1024,512]{1,0:T(8,128)(2,1)S(1)} collective-permute-done((bf16[1024,512]{1,0:T(8,128)(2,1)S(1)}, bf16[1024,512]{1,0:T(8,128)(2,1)S(1)}, u32[]{:S(2)}, u32[]{:S(2)}) %collective-permute-start.19) | collective-permute-done | bytes 1048608 | tf_op jit(solution)/shard_map/g_far/ppermute | solution.py:306
  88.5 2.6 %collective-permute-start.20 = (bf16[1024,512]{1,0:T(8,128)(2,1)S(1)}, bf16[1024,512]{1,0:T(8,128)(2,1)S(1)}, u32[]{:S(2)}, u32[]{:S(2)}) collective-permute-start(bf16[1024,512]{1,0:T(8,128)(2,1)S(1)} %collective-permute-done.19.refs_0_), channel_id=1, source_target_pairs={{0,1},{1,0},{2,3},{3,2},{4,5},{5,4},{6,7},{7,6},{8,9},{9,8},{10,11... | collective-permute-start | bytes 3145736 | tf_op jit(solution)/shard_map/swap_far/ppermute | solution.py:306
  91.1 2.1 %shard_map.139 = (f32[256,512]{1,0:T(8,128)}, f32[256,512]{1,0:T(8,128)}, f32[256,512]{1,0:T(8,128)}, f32[32,128]{1,0:T(8,128)}, f32[32,128]{1,0:T(8,128)}) custom-call(s32[2]{0:T(128)S(1)} %pad_add_fusion.place, bf16[512,256]{1,0:T(8,128)(2,1)S(1)} %get-tuple-element.194.own, bf16[512,256]{1,0:T(8,128)(2,1)S(1)} %collective-permute-done.17.one, ...), custom_call_target="tpu_custom_call" | custom-call | flops 1 | bytes 1 | tf_op jit(solution)/shard_map/pallas_call | solution.py:283
  93.3 0.1 collective-permute-done.20.refs_1_
  93.4 2.1 %shard_map.140 = bf16[256,8192]{1,0:T(8,128)(2,1)} custom-call(s32[32]{0:T(128)S(1)} %stack.137.table, bf16[256,512]{1,0:T(8,128)(2,1)S(1)} %bitcast.48, bf16[1024,512]{1,0:T(8,128)(2,1)S(1)} %collective-permute-done.19.refs_0_, bf16[1024,512]{1,0:T(8,128)(2,1)S(1)} %collective-permute-done.20.refs_1_, ...), custom_call_target="tpu_custom_call", output_to_operand_aliasing={{}: (4, {})} | custom-call | flops 1 | bytes 1 | tf_op jit(solution)/shard_map/pallas_call | solution.py:220
  (34 shorter events, 0.2 us)
Async XLA Ops:
  1.1 1.0 copy-start.1
  2.0 2.2 %copy-start.3 = (bf16[1,256,8192]{2,1,0:T(8,128)(2,1)S(1)}, bf16[1,256,8192]{2,1,0:T(8,128)(2,1)}, u32[]{:S(2)}) copy-start(bf16[1,256,8192]{2,1,0:T(8,128)(2,1)} %param.8) | copy-start | bytes 12582916
  5.4 11.3 %copy-start = (f32[1,256,512]{2,1,0:T(8,128)S(1)}, f32[1,256,512]{2,1,0:T(8,128)}, u32[]{:S(2)}) copy-start(f32[1,256,512]{2,1,0:T(8,128)} %param.10) | copy-start | bytes 1572868
  5.4 5.2 %collective-permute-start = (bf16[6,256,256]{2,1,0:T(8,128)(2,1)S(1)}, bf16[6,256,256]{2,1,0:T(8,128)(2,1)S(1)}, u32[]{:S(2)}, u32[]{:S(2)}) collective-permute-start(bf16[6,256,256]{2,1,0:T(8,128)(2,1)S(1)} %get-tuple-element.114), channel_id=1, source_target_pairs={{0,1},{1,0},{2,3},{3,2},{4,5},{5,4},{6,7},{7,6},{8,9},{9,8},{10,11... | collective-permute-start | bytes 2359304 | tf_op jit(solution)/shard_map/swap_inputs/ppermute | solution.py:306
  10.6 3.4 %collective-permute-start.1 = (bf16[12,256,256]{2,1,0:T(8,128)(2,1)S(1)}, bf16[12,256,256]{2,1,0:T(8,128)(2,1)S(1)}, u32[]{:S(2)}, u32[]{:S(2)}) collective-permute-start(bf16[12,256,256]{2,1,0:T(8,128)(2,1)S(1)} %get-tuple-element.121), channel_id=1, source_target_pairs={{0,1},{1,0},{2,3},{3,2},{4,5},{5,4},{6,7},{7,6},{8,9},{9,8},{10,11... | collective-permute-start | bytes 4718600 | tf_op jit(solution)/shard_map/swap_inputs_late/ppermute | solution.py:306
  11.7 20.7 %collective-permute-start.4 = (bf16[4,512,256]{2,1,0:T(8,128)(2,1)S(1)}, bf16[4,512,256]{2,1,0:T(8,128)(2,1)S(1)}, u32[]{:S(2)}, u32[]{:S(2)}) collective-permute-start(bf16[4,512,256]{2,1,0:T(8,128)(2,1)S(1)} %shard_map.128), channel_id=1, source_target_pairs={{0,2},{1,7},{2,4},{3,1},{4,6},{5,3},{6,0},{7,5},{8,10},{9,15},{10,... | collective-permute-start | bytes 3145736 | tf_op jit(solution)/shard_map/r_far/ppermute | solution.py:306
  16.7 25.1 %copy-start.4 = (bf16[4,512,256]{2,1,0:T(8,128)(2,1)}, bf16[4,512,256]{2,1,0:T(8,128)(2,1)S(1)}, u32[]{:S(2)}) copy-start(bf16[4,512,256]{2,1,0:T(8,128)(2,1)S(1)} %get-tuple-element.146.refs_0_) | copy-start | bytes 3145732
  16.7 28.6 %collective-permute-start.6 = (bf16[4,512,256]{2,1,0:T(8,128)(2,1)}, bf16[4,512,256]{2,1,0:T(8,128)(2,1)}, u32[]{:S(2)}, u32[]{:S(2)}) collective-permute-start(bf16[4,512,256]{2,1,0:T(8,128)(2,1)} %get-tuple-element.144), channel_id=1, source_target_pairs={{0,6},{1,3},{2,0},{3,5},{4,2},{5,7},{6,4},{7,1},{8,14},{9,11},{10,... | collective-permute-start | bytes 3145736 | tf_op jit(solution)/shard_map/r_back/ppermute | solution.py:306
  16.7 31.2 %copy-start.8 = (f32[32,128]{1,0:T(8,128)S(1)}, f32[32,128]{1,0:T(8,128)}, u32[]{:S(2)}) copy-start(f32[32,128]{1,0:T(8,128)} %outer.3) | copy-start | bytes 49156
  16.7 31.2 %copy-start.9 = (f32[32,128]{1,0:T(8,128)S(1)}, f32[32,128]{1,0:T(8,128)}, u32[]{:S(2)}) copy-start(f32[32,128]{1,0:T(8,128)} %momentum.3) | copy-start | bytes 49156
  16.7 10.1 %collective-permute-start.2 = (bf16[256,512]{1,0:T(8,128)(2,1)S(1)}, bf16[256,512]{1,0:T(8,128)(2,1)S(1)}, u32[]{:S(2)}, u32[]{:S(2)}) collective-permute-start(bf16[256,512]{1,0:T(8,128)(2,1)S(1)} %shard_map.130.refs_0_), channel_id=1, source_target_pairs={{0,8},{1,25},{2,10},{3,27},{4,12},{5,29},{6,14},{7,31},{8,16},{9,1... | collective-permute-start | bytes 786440 | tf_op jit(solution)/shard_map/z_on/ppermute | solution.py:306
  20.7 11.7 %collective-permute-start.3 = (bf16[256,512]{1,0:T(8,128)(2,1)S(1)}, bf16[256,512]{1,0:T(8,128)(2,1)S(1)}, u32[]{:S(2)}, u32[]{:S(2)}) collective-permute-start(bf16[256,512]{1,0:T(8,128)(2,1)S(1)} %shard_map.130.refs_0_), channel_id=1, source_target_pairs={{0,24},{1,9},{2,26},{3,11},{4,28},{5,13},{6,30},{7,15},{8,0},{9,17... | collective-permute-start | bytes 786440 | tf_op jit(solution)/shard_map/z_back/ppermute | solution.py:306
  32.4 9.2 %collective-permute-start.5 = (bf16[256,512]{1,0:T(8,128)(2,1)S(1)}, bf16[256,512]{1,0:T(8,128)(2,1)S(1)}, u32[]{:S(2)}, u32[]{:S(2)}) collective-permute-start(bf16[256,512]{1,0:T(8,128)(2,1)S(1)} %collective-permute-done.2.refs_1_), channel_id=1, source_target_pairs={{0,8},{1,25},{2,10},{3,27},{4,12},{5,29},{6,14},{7,31},{8,16},{9,1... | collective-permute-start | bytes 786440 | tf_op jit(solution)/shard_map/z_far/ppermute | solution.py:306
  33.6 27.8 %collective-permute-start.9 = (bf16[4,512,256]{2,1,0:T(8,128)(2,1)}, bf16[4,512,256]{2,1,0:T(8,128)(2,1)}, u32[]{:S(2)}, u32[]{:S(2)}) collective-permute-start(bf16[4,512,256]{2,1,0:T(8,128)(2,1)} %shard_map.131), channel_id=1, source_target_pairs={{0,2},{1,7},{2,4},{3,1},{4,6},{5,3},{6,0},{7,5},{8,10},{9,15},{10,... | collective-permute-start | bytes 3145736 | tf_op jit(solution)/shard_map/r_on/ppermute | solution.py:306
  41.6 36.8 %copy-start.2 = (bf16[1,256,512]{2,1,0:T(8,128)(2,1)S(1)}, bf16[1,256,512]{2,1,0:T(8,128)(2,1)}, u32[]{:S(2)}) copy-start(bf16[1,256,512]{2,1,0:T(8,128)(2,1)} %param.9) | copy-start | bytes 786436
  41.7 24.7 %collective-permute-start.10 = (bf16[1024,512]{1,0:T(8,128)(2,1)S(1)}, bf16[1024,512]{1,0:T(8,128)(2,1)}, u32[]{:S(2)}, u32[]{:S(2)}) collective-permute-start(bf16[1024,512]{1,0:T(8,128)(2,1)S(1)} %shard_map.132.refs_0_), channel_id=1, source_target_pairs={{0,1},{1,0},{2,3},{3,2},{4,5},{5,4},{6,7},{7,6},{8,9},{9,8},{10,11... | collective-permute-start | bytes 3145736 | tf_op jit(solution)/shard_map/swap_near/ppermute | solution.py:306
  41.8 31.0 %collective-permute-start.14 = (bf16[1024,512]{1,0:T(8,128)(2,1)S(1)}, bf16[1024,512]{1,0:T(8,128)(2,1)}, u32[]{:S(2)}, u32[]{:S(2)}) collective-permute-start(bf16[1024,512]{1,0:T(8,128)(2,1)S(1)} %shard_map.132.refs_0_), channel_id=1, source_target_pairs={{0,6},{1,3},{2,0},{3,5},{4,2},{5,7},{6,4},{7,1},{8,14},{9,11},{10,... | collective-permute-start | bytes 3145736 | tf_op jit(solution)/shard_map/g_back/ppermute | solution.py:306
  43.5 29.3 %collective-permute-start.13 = (bf16[1024,512]{1,0:T(8,128)(2,1)S(1)}, bf16[1024,512]{1,0:T(8,128)(2,1)S(1)}, u32[]{:S(2)}, u32[]{:S(2)}) collective-permute-start(bf16[1024,512]{1,0:T(8,128)(2,1)S(1)} %shard_map.132.refs_0_), channel_id=1, source_target_pairs={{0,2},{1,7},{2,4},{3,1},{4,6},{5,3},{6,0},{7,5},{8,10},{9,15},{10,... | collective-permute-start | bytes 3145736 | tf_op jit(solution)/shard_map/g_on/ppermute | solution.py:306
  45.3 1.2 %copy-start.5 = (bf16[4,512,256]{2,1,0:T(8,128)(2,1)S(1)}, bf16[4,512,256]{2,1,0:T(8,128)(2,1)}, u32[]{:S(2)}) copy-start(bf16[4,512,256]{2,1,0:T(8,128)(2,1)} %copy-done.4) | copy-start | bytes 3145732
  48.7 7.9 %collective-permute-start.7 = (bf16[256,128]{1,0:T(8,128)(2,1)S(1)}, bf16[256,128]{1,0:T(8,128)(2,1)S(1)}, u32[]{:S(2)}, u32[]{:S(2)}) collective-permute-start(bf16[256,128]{1,0:T(8,128)(2,1)S(1)} %convert_element_type.6), channel_id=1, source_target_pairs={{0,128},{32,160},{64,192},{96,224},{128,0},{160,32},{192,64},{224,... | collective-permute-start | bytes 196616 | tf_op jit(solution)/shard_map/frag_h/ppermute | solution.py:310
  56.6 4.8 %collective-permute-start.8 = (f32[256,128]{1,0:T(8,128)S(1)}, f32[256,128]{1,0:T(8,128)S(1)}, u32[]{:S(2)}, u32[]{:S(2)}) collective-permute-start(f32[256,128]{1,0:T(8,128)S(1)} %convert_add_fusion), channel_id=1, source_target_pairs={{0,32},{32,0},{64,96},{96,64},{128,160},{160,128},{192,224},{224,1... | collective-permute-start | bytes 393224 | tf_op jit(solution)/shard_map/frag_x1/ppermute | solution.py:310
  62.9 9.9 %collective-permute-start.12 = (bf16[512,256]{1,0:T(8,128)(2,1)S(1)}, bf16[512,256]{1,0:T(8,128)(2,1)S(1)}, u32[]{:S(2)}, u32[]{:S(2)}) collective-permute-start(bf16[512,256]{1,0:T(8,128)(2,1)S(1)} %get-tuple-element.175), channel_id=1, source_target_pairs={{0,8},{1,25},{2,10},{3,27},{4,12},{5,29},{6,14},{7,31},{8,16},{9,1... | collective-permute-start | bytes 786440 | tf_op jit(solution)/shard_map/rz_far/ppermute | solution.py:306
  63.9 5.3 %collective-permute-start.11 = (f32[256,128]{1,0:T(8,128)S(1)}, f32[256,128]{1,0:T(8,128)S(1)}, u32[]{:S(2)}, u32[]{:S(2)}) collective-permute-start(f32[256,128]{1,0:T(8,128)S(1)} %add.487), channel_id=1, source_target_pairs={{0,96},{32,64},{64,32},{96,0},{128,224},{160,192},{192,160},{224,1... | collective-permute-start | bytes 393224 | tf_op jit(solution)/shard_map/frag_x2/ppermute | solution.py:310
  72.8 5.6 %collective-permute-start.16 = (bf16[1024,512]{1,0:T(8,128)(2,1)}, bf16[1024,512]{1,0:T(8,128)(2,1)S(1)}, u32[]{:S(2)}, u32[]{:S(2)}) collective-permute-start(bf16[1024,512]{1,0:T(8,128)(2,1)} %collective-permute-done.14.refs_2_), channel_id=1, source_target_pairs={{0,1},{1,0},{2,3},{3,2},{4,5},{5,4},{6,7},{7,6},{8,9},{9,8},{10,11... | collective-permute-start | bytes 3145736 | tf_op jit(solution)/shard_map/swap_back/ppermute | solution.py:306
  74.5 4.0 %collective-permute-start.15 = (bf16[1024,512]{1,0:T(8,128)(2,1)S(1)}, bf16[1024,512]{1,0:T(8,128)(2,1)S(1)}, u32[]{:S(2)}, u32[]{:S(2)}) collective-permute-start(bf16[1024,512]{1,0:T(8,128)(2,1)S(1)} %collective-permute-done.13.refs_0_), channel_id=1, source_target_pairs={{0,1},{1,0},{2,3},{3,2},{4,5},{5,4},{6,7},{7,6},{8,9},{9,8},{10,11... | collective-permute-start | bytes 3145736 | tf_op jit(solution)/shard_map/swap_on/ppermute | solution.py:306
  74.5 13.9 %collective-permute-start.19 = (bf16[1024,512]{1,0:T(8,128)(2,1)S(1)}, bf16[1024,512]{1,0:T(8,128)(2,1)S(1)}, u32[]{:S(2)}, u32[]{:S(2)}) collective-permute-start(bf16[1024,512]{1,0:T(8,128)(2,1)S(1)} %collective-permute-done.13.refs_0_), channel_id=1, source_target_pairs={{0,2},{1,7},{2,4},{3,1},{4,6},{5,3},{6,0},{7,5},{8,10},{9,15},{10,... | collective-permute-start | bytes 3145736 | tf_op jit(solution)/shard_map/g_far/ppermute | solution.py:306
  74.9 9.8 %collective-permute-start.17 = (bf16[512,256]{1,0:T(8,128)(2,1)S(1)}, bf16[512,256]{1,0:T(8,128)(2,1)S(1)}, u32[]{:S(2)}, u32[]{:S(2)}) collective-permute-start(bf16[512,256]{1,0:T(8,128)(2,1)S(1)} %get-tuple-element.190), channel_id=1, source_target_pairs={{0,24},{1,9},{2,26},{3,11},{4,28},{5,13},{6,30},{7,15},{8,0},{9,17... | collective-permute-start | bytes 786440 | tf_op jit(solution)/shard_map/rz_back/ppermute | solution.py:306
  75.5 11.7 %collective-permute-start.18 = (bf16[512,256]{1,0:T(8,128)(2,1)S(1)}, bf16[512,256]{1,0:T(8,128)(2,1)S(1)}, u32[]{:S(2)}, u32[]{:S(2)}) collective-permute-start(bf16[512,256]{1,0:T(8,128)(2,1)S(1)} %shard_map.136), channel_id=1, source_target_pairs={{0,8},{1,25},{2,10},{3,27},{4,12},{5,29},{6,14},{7,31},{8,16},{9,1... | collective-permute-start | bytes 786440 | tf_op jit(solution)/shard_map/rz_on/ppermute | solution.py:306
  81.9 9.2 %copy-start.6 = (f32[1,256,512]{2,1,0:T(8,128)S(1)}, f32[1,256,512]{2,1,0:T(8,128)}, u32[]{:S(2)}) copy-start(f32[1,256,512]{2,1,0:T(8,128)} %param.11) | copy-start | bytes 1572868
  81.9 9.2 %copy-start.7 = (f32[1,256,512]{2,1,0:T(8,128)S(1)}, f32[1,256,512]{2,1,0:T(8,128)}, u32[]{:S(2)}) copy-start(f32[1,256,512]{2,1,0:T(8,128)} %param.12) | copy-start | bytes 1572868
  88.5 4.9 %collective-permute-start.20 = (bf16[1024,512]{1,0:T(8,128)(2,1)S(1)}, bf16[1024,512]{1,0:T(8,128)(2,1)S(1)}, u32[]{:S(2)}, u32[]{:S(2)}) collective-permute-start(bf16[1024,512]{1,0:T(8,128)(2,1)S(1)} %collective-permute-done.19.refs_0_), channel_id=1, source_target_pairs={{0,1},{1,0},{2,3},{3,2},{4,5},{5,4},{6,7},{7,6},{8,9},{9,8},{10,11... | collective-permute-start | bytes 3145736 | tf_op jit(solution)/shard_map/swap_far/ppermute | solution.py:306

commit v3 on v2

--- a/solution.py
+++ b/solution.py
@@ -372,13 +372,13 @@
     ga = send(near, ON_Y, "g_on")
     gb = send(near, BACK_Y, "g_back")
     near_back = tie(near_back)
-    part_own = tie(*add(part_own, near_back))
 
     mix = tie(mix_start(place, slope, islands, tie(master), outer_params, outer_momentum))
     mix_x = send_island(mix.astype(BF16), SWAP_H, "frag_h")
     mix_x = tie(mix_x)
     mix = tie(mix + mix_x.astype(F32))
     mix_x = send_island(mix, PAIR_X, "frag_x1")
+    part_own = tie(*add(part_own, near_back))
     mix_x = tie(mix_x)
     mix = tie(mix + mix_x)
     mix_x = send_island(mix, CROSS_X, "frag_x2")

time: 96 us -> 96 us (level)
    ppermute x3, waiting for transfers between devices: 9.04 us -> 6.35 us  [send_island(): return lax.ppermute(value, 'island', pairs)]
    ppermute x18, waiting for transfers between devices: 27.1 us -> 29.5 us  [send(): return lax.ppermute(value, 'fsdp', pairs)]
  transfers between devices with their start and end apart: 21 -> 21, of which waited for: 13 -> 14; matrix products, arithmetic and copies ran while one was open for 0% -> 0% of each run, Pallas kernels for 18% -> 18%
where the time goes in v3:
time: 96 us; the launch traced here: 95.6 us
  waiting for transfers between devices  35.8 us (37%)
  starting transfers between devices  33.2 us (35%)
  Pallas kernels  20 us (21%)
  local copies, waits for them, and re-layouts  4.51 us (5%)
  between operations  1.96 us (2%)
    ppermute x18, waiting for transfers between devices, send(): return lax.ppermute(value, 'fsdp', pairs)  29.5 us
    ppermute x18, starting transfers between devices, send(): return lax.ppermute(value, 'fsdp', pairs)  24.3 us
    ppermute x3, starting transfers between devices, send_island(): return lax.ppermute(value, 'island', pairs)  8.92 us
    pallas_call x3, Pallas kernels, input_blocks(): pl.pallas_call(body, out_shape=jax.ShapeDtypeStruct((cotan.shape[0], widt...  8.33 us
    ppermute x3, waiting for transfers between devices, send_island(): return lax.ppermute(value, 'island', pairs)  6.35 us
    unnamed x20, local copies, waits for them, and re-layouts  4.39 us
    pallas_call x3, Pallas kernels, add(): pl.pallas_call(body, out_shape=[jax.ShapeDtypeStruct(tuple(shape), BF16)...  4.15 us
    pallas_call x2, Pallas kernels, grad_blocks(): pl.pallas_call(body, out_shape=[jax.ShapeDtypeStruct((NZ, halves * width,...  3.34 us
  transfers between devices with their start and end apart: 21, of which 14 were waited for; matrix products, arithmetic and copies ran while one was open for 0% of the time, Pallas kernels for 18%

profile of v3, /device:TPU:1, one launch (start us, length us, event | category | flops | bytes accessed | tf_op | source)
XLA Modules:
  0.0 95.6 jit_solution(3998180468871709696)
XLA Ops:
  0.9 0.1 stack.137.table
  1.1 0.9 copy-done.1
  2.0 2.2 %copy-done.3 = bf16[1,256,8192]{2,1,0:T(8,128)(2,1)S(1)} copy-done((bf16[1,256,8192]{2,1,0:T(8,128)(2,1)S(1)}, bf16[1,256,8192]{2,1,0:T(8,128)(2,1)}, u32[]{:S(2)}) %copy-start.3) | copy-done | bytes 4194328
  4.2 1.2 %shard_map.127 = (bf16[6,256,256]{2,1,0:T(8,128)(2,1)S(1)}, bf16[12,256,256]{2,1,0:T(8,128)(2,1)S(1)}, bf16[18,256,256]{2,1,0:T(8,128)(2,1)S(1)}) custom-call(s32[32]{0:T(128)S(1)} %stack.137.table, bf16[256,8192]{1,0:T(8,128)(2,1)S(1)} %bitcast.49, bf16[256,512]{1,0:T(8,128)(2,1)S(1)} %bitcast.45), custom_call_target="tpu_custom_call" | custom-call | flops 1 | bytes 1 | tf_op jit(solution)/shard_map/pallas_call | solution.py:96
  5.4 3.3 %collective-permute-start = (bf16[6,256,256]{2,1,0:T(8,128)(2,1)S(1)}, bf16[6,256,256]{2,1,0:T(8,128)(2,1)S(1)}, u32[]{:S(2)}, u32[]{:S(2)}) collective-permute-start(bf16[6,256,256]{2,1,0:T(8,128)(2,1)S(1)} %get-tuple-element.114), channel_id=1, source_target_pairs={{0,1},{1,0},{2,3},{3,2},{4,5},{5,4},{6,7},{7,6},{8,9},{9,8},{10,11... | collective-permute-start | bytes 2359304 | tf_op jit(solution)/shard_map/swap_inputs/ppermute | solution.py:306
  8.7 1.9 %collective-permute-done.swapped.packed = bf16[6,256,256]{2,1,0:T(8,128)(2,1)S(1)} collective-permute-done((bf16[6,256,256]{2,1,0:T(8,128)(2,1)S(1)}, bf16[6,256,256]{2,1,0:T(8,128)(2,1)S(1)}, u32[]{:S(2)}, u32[]{:S(2)}) %collective-permute-start) | collective-permute-done | bytes 786464 | tf_op jit(solution)/shard_map/swap_inputs/ppermute | solution.py:306
  10.6 0.4 collective-permute-start.1
  11.0 0.7 shard_map.128
  11.7 1.1 %collective-permute-start.4 = (bf16[4,512,256]{2,1,0:T(8,128)(2,1)S(1)}, bf16[4,512,256]{2,1,0:T(8,128)(2,1)S(1)}, u32[]{:S(2)}, u32[]{:S(2)}) collective-permute-start(bf16[4,512,256]{2,1,0:T(8,128)(2,1)S(1)} %shard_map.128), channel_id=1, source_target_pairs={{0,2},{1,7},{2,4},{3,1},{4,6},{5,3},{6,0},{7,5},{8,10},{9,15},{10,... | collective-permute-start | bytes 3145736 | tf_op jit(solution)/shard_map/r_far/ppermute | solution.py:306
  12.8 1.2 %collective-permute-done.1.packed = bf16[12,256,256]{2,1,0:T(8,128)(2,1)S(1)} collective-permute-done((bf16[12,256,256]{2,1,0:T(8,128)(2,1)S(1)}, bf16[12,256,256]{2,1,0:T(8,128)(2,1)S(1)}, u32[]{:S(2)}, u32[]{:S(2)}) %collective-permute-start.1) | collective-permute-done | bytes 1572896 | tf_op jit(solution)/shard_map/swap_inputs_late/ppermute | solution.py:306
  14.0 2.6 %shard_map.129 = (bf16[4,512,256]{2,1,0:T(8,128)(2,1)}, bf16[4,512,256]{2,1,0:T(8,128)(2,1)S(1)}, bf16[4,512,256]{2,1,0:T(8,128)(2,1)S(1)}) custom-call(bf16[18,256,256]{2,1,0:T(8,128)(2,1)S(1)} %get-tuple-element.118.own, bf16[6,256,256]{2,1,0:T(8,128)(2,1)S(1)} %collective-permute-done.swapped.packed, bf16[12,256,256]{2,1,0:T(8,128)(2,1)S(1)} %collective-permute-done.1.packed), custom_call_target="tpu_custom_call" | custom-call | flops 1 | bytes 1 | tf_op jit(solution)/shard_map/pallas_call | solution.py:142
  16.7 4.0 %collective-permute-start.2 = (bf16[256,512]{1,0:T(8,128)(2,1)S(1)}, bf16[256,512]{1,0:T(8,128)(2,1)S(1)}, u32[]{:S(2)}, u32[]{:S(2)}) collective-permute-start(bf16[256,512]{1,0:T(8,128)(2,1)S(1)} %shard_map.130.refs_0_), channel_id=1, source_target_pairs={{0,8},{1,25},{2,10},{3,27},{4,12},{5,29},{6,14},{7,31},{8,16},{9,1... | collective-permute-start | bytes 786440 | tf_op jit(solution)/shard_map/z_on/ppermute | solution.py:306
  20.7 6.1 %collective-permute-done.2.refs_1_ = bf16[256,512]{1,0:T(8,128)(2,1)S(1)} collective-permute-done((bf16[256,512]{1,0:T(8,128)(2,1)S(1)}, bf16[256,512]{1,0:T(8,128)(2,1)S(1)}, u32[]{:S(2)}, u32[]{:S(2)}) %collective-permute-start.2) | collective-permute-done | bytes 262176 | tf_op jit(solution)/shard_map/z_on/ppermute | solution.py:306
  26.8 5.5 %collective-permute-done.3.refs_2_ = bf16[256,512]{1,0:T(8,128)(2,1)S(1)} collective-permute-done((bf16[256,512]{1,0:T(8,128)(2,1)S(1)}, bf16[256,512]{1,0:T(8,128)(2,1)S(1)}, u32[]{:S(2)}, u32[]{:S(2)}) %collective-permute-start.3) | collective-permute-done | bytes 262176 | tf_op jit(solution)/shard_map/z_back/ppermute | solution.py:306
  32.4 1.2 %shard_map.131 = bf16[4,512,256]{2,1,0:T(8,128)(2,1)} custom-call(bf16[4,512,256]{2,1,0:T(8,128)(2,1)S(1)} %get-tuple-element.136.refs_0_, bf16[4,512,256]{2,1,0:T(8,128)(2,1)S(1)} %collective-permute-done.4.refs_1_), custom_call_target="tpu_custom_call" | custom-call | flops 1 | bytes 1 | tf_op jit(solution)/shard_map/pallas_call | solution.py:167
  33.6 3.3 %collective-permute-start.9 = (bf16[4,512,256]{2,1,0:T(8,128)(2,1)}, bf16[4,512,256]{2,1,0:T(8,128)(2,1)}, u32[]{:S(2)}, u32[]{:S(2)}) collective-permute-start(bf16[4,512,256]{2,1,0:T(8,128)(2,1)} %shard_map.131), channel_id=1, source_target_pairs={{0,2},{1,7},{2,4},{3,1},{4,6},{5,3},{6,0},{7,5},{8,10},{9,15},{10,... | collective-permute-start | bytes 3145736 | tf_op jit(solution)/shard_map/r_on/ppermute | solution.py:306
  36.9 4.7 %collective-permute-done.5.refs_3_ = bf16[256,512]{1,0:T(8,128)(2,1)S(1)} collective-permute-done((bf16[256,512]{1,0:T(8,128)(2,1)S(1)}, bf16[256,512]{1,0:T(8,128)(2,1)S(1)}, u32[]{:S(2)}, u32[]{:S(2)}) %collective-permute-start.5) | collective-permute-done | bytes 262176 | tf_op jit(solution)/shard_map/z_far/ppermute | solution.py:306
  41.6 0.1 shard_map.132.refs_0_
  41.6 0.1 collective-permute-start.10
  41.8 1.7 %collective-permute-start.14 = (bf16[1024,512]{1,0:T(8,128)(2,1)S(1)}, bf16[1024,512]{1,0:T(8,128)(2,1)}, u32[]{:S(2)}, u32[]{:S(2)}) collective-permute-start(bf16[1024,512]{1,0:T(8,128)(2,1)S(1)} %shard_map.132.refs_0_), channel_id=1, source_target_pairs={{0,6},{1,3},{2,0},{3,5},{4,2},{5,7},{6,4},{7,1},{8,14},{9,11},{10,... | collective-permute-start | bytes 3145736 | tf_op jit(solution)/shard_map/g_back/ppermute | solution.py:306
  43.5 1.0 %collective-permute-start.13 = (bf16[1024,512]{1,0:T(8,128)(2,1)S(1)}, bf16[1024,512]{1,0:T(8,128)(2,1)S(1)}, u32[]{:S(2)}, u32[]{:S(2)}) collective-permute-start(bf16[1024,512]{1,0:T(8,128)(2,1)S(1)} %shard_map.132.refs_0_), channel_id=1, source_target_pairs={{0,2},{1,7},{2,4},{3,1},{4,6},{5,3},{6,0},{7,5},{8,10},{9,15},{10,... | collective-permute-start | bytes 3145736 | tf_op jit(solution)/shard_map/g_on/ppermute | solution.py:306
  45.2 0.1 pad_add_fusion.place
  45.2 0.7 shard_map.133
  46.0 5.0 %collective-permute-start.7 = (bf16[256,128]{1,0:T(8,128)(2,1)S(1)}, bf16[256,128]{1,0:T(8,128)(2,1)S(1)}, u32[]{:S(2)}, u32[]{:S(2)}) collective-permute-start(bf16[256,128]{1,0:T(8,128)(2,1)S(1)} %convert_element_type.6), channel_id=1, source_target_pairs={{0,128},{32,160},{64,192},{96,224},{128,0},{160,32},{192,64},{224,... | collective-permute-start | bytes 196616 | tf_op jit(solution)/shard_map/frag_h/ppermute | solution.py:310
  51.0 2.9 %collective-permute-done.7 = bf16[256,128]{1,0:T(8,128)(2,1)S(1)} collective-permute-done((bf16[256,128]{1,0:T(8,128)(2,1)S(1)}, bf16[256,128]{1,0:T(8,128)(2,1)S(1)}, u32[]{:S(2)}, u32[]{:S(2)}) %collective-permute-start.7) | collective-permute-done | bytes 65568 | tf_op jit(solution)/shard_map/frag_h/ppermute | solution.py:310
  53.9 1.5 %collective-permute-start.8 = (f32[256,128]{1,0:T(8,128)S(1)}, f32[256,128]{1,0:T(8,128)S(1)}, u32[]{:S(2)}, u32[]{:S(2)}) collective-permute-start(f32[256,128]{1,0:T(8,128)S(1)} %convert_add_fusion), channel_id=1, source_target_pairs={{0,32},{32,0},{64,96},{96,64},{128,160},{160,128},{192,224},{224,1... | collective-permute-start | bytes 393224 | tf_op jit(solution)/shard_map/frag_x1/ppermute | solution.py:310
  55.4 1.2 %copy-done.5 = bf16[4,512,256]{2,1,0:T(8,128)(2,1)S(1)} copy-done((bf16[4,512,256]{2,1,0:T(8,128)(2,1)S(1)}, bf16[4,512,256]{2,1,0:T(8,128)(2,1)}, u32[]{:S(2)}) %copy-start.5) | copy-done | bytes 1048600
  56.6 1.5 %shard_map.134.refs_0_ = bf16[4,512,256]{2,1,0:T(8,128)(2,1)S(1)} custom-call(bf16[4,512,256]{2,1,0:T(8,128)(2,1)S(1)} %copy-done.5, bf16[4,512,256]{2,1,0:T(8,128)(2,1)} %collective-permute-done.6.refs_1_), custom_call_target="tpu_custom_call" | custom-call | flops 1 | bytes 1 | tf_op jit(solution)/shard_map/pallas_call | solution.py:167
  58.1 0.6 collective-permute-done.8
  58.7 1.5 %shard_map.135 = (bf16[512,256]{1,0:T(8,128)(2,1)S(1)}, bf16[512,256]{1,0:T(8,128)(2,1)S(1)}, bf16[512,256]{1,0:T(8,128)(2,1)S(1)}, bf16[512,256]{1,0:T(8,128)(2,1)S(1)}) custom-call(bf16[4,512,256]{2,1,0:T(8,128)(2,1)S(1)} %shard_map.134.refs_0_, bf16[4,512,256]{2,1,0:T(8,128)(2,1)} %collective-permute-done.9.refs_1_), custom_call_target="tpu_custom_call" | custom-call | flops 1 | bytes 1 | tf_op jit(solution)/shard_map/pallas_call | solution.py:167
  60.2 1.0 %collective-permute-start.12 = (bf16[512,256]{1,0:T(8,128)(2,1)S(1)}, bf16[512,256]{1,0:T(8,128)(2,1)S(1)}, u32[]{:S(2)}, u32[]{:S(2)}) collective-permute-start(bf16[512,256]{1,0:T(8,128)(2,1)S(1)} %get-tuple-element.175), channel_id=1, source_target_pairs={{0,8},{1,25},{2,10},{3,27},{4,12},{5,29},{6,14},{7,31},{8,16},{9,1... | collective-permute-start | bytes 786440 | tf_op jit(solution)/shard_map/rz_far/ppermute | solution.py:306
  61.2 2.5 %collective-permute-start.11 = (f32[256,128]{1,0:T(8,128)S(1)}, f32[256,128]{1,0:T(8,128)S(1)}, u32[]{:S(2)}, u32[]{:S(2)}) collective-permute-start(f32[256,128]{1,0:T(8,128)S(1)} %add.487), channel_id=1, source_target_pairs={{0,96},{32,64},{64,32},{96,0},{128,224},{160,192},{192,160},{224,1... | collective-permute-start | bytes 393224 | tf_op jit(solution)/shard_map/frag_x2/ppermute | solution.py:310
  63.6 2.8 %collective-permute-done.11 = f32[256,128]{1,0:T(8,128)S(1)} collective-permute-done((f32[256,128]{1,0:T(8,128)S(1)}, f32[256,128]{1,0:T(8,128)S(1)}, u32[]{:S(2)}, u32[]{:S(2)}) %collective-permute-start.11) | collective-permute-done | bytes 131104 | tf_op jit(solution)/shard_map/frag_x2/ppermute | solution.py:310
  66.5 3.5 %collective-permute-done.12.b = bf16[512,256]{1,0:T(8,128)(2,1)S(1)} collective-permute-done((bf16[512,256]{1,0:T(8,128)(2,1)S(1)}, bf16[512,256]{1,0:T(8,128)(2,1)S(1)}, u32[]{:S(2)}, u32[]{:S(2)}) %collective-permute-start.12) | collective-permute-done | bytes 262176 | tf_op jit(solution)/shard_map/rz_far/ppermute | solution.py:306
  70.1 2.3 %collective-permute-done.13.refs_0_ = bf16[1024,512]{1,0:T(8,128)(2,1)S(1)} collective-permute-done((bf16[1024,512]{1,0:T(8,128)(2,1)S(1)}, bf16[1024,512]{1,0:T(8,128)(2,1)S(1)}, u32[]{:S(2)}, u32[]{:S(2)}) %collective-permute-start.13) | collective-permute-done | bytes 1048608 | tf_op jit(solution)/shard_map/g_on/ppermute | solution.py:306
  72.4 2.1 %collective-permute-start.16 = (bf16[1024,512]{1,0:T(8,128)(2,1)}, bf16[1024,512]{1,0:T(8,128)(2,1)S(1)}, u32[]{:S(2)}, u32[]{:S(2)}) collective-permute-start(bf16[1024,512]{1,0:T(8,128)(2,1)} %collective-permute-done.14.refs_2_), channel_id=1, source_target_pairs={{0,1},{1,0},{2,3},{3,2},{4,5},{5,4},{6,7},{7,6},{8,9},{9,8},{10,11... | collective-permute-start | bytes 3145736 | tf_op jit(solution)/shard_map/swap_back/ppermute | solution.py:306
  74.5 0.4 collective-permute-start.19
  74.9 0.6 collective-permute-start.17
  75.5 2.7 %collective-permute-start.18 = (bf16[512,256]{1,0:T(8,128)(2,1)S(1)}, bf16[512,256]{1,0:T(8,128)(2,1)S(1)}, u32[]{:S(2)}, u32[]{:S(2)}) collective-permute-start(bf16[512,256]{1,0:T(8,128)(2,1)S(1)} %shard_map.136), channel_id=1, source_target_pairs={{0,8},{1,25},{2,10},{3,27},{4,12},{5,29},{6,14},{7,31},{8,16},{9,1... | collective-permute-start | bytes 786440 | tf_op jit(solution)/shard_map/rz_on/ppermute | solution.py:306
  78.2 0.3 collective-permute-done.16.refs_3_
  78.5 3.4 %shard_map.137.refs_2_ = bf16[256,8192]{1,0:T(8,128)(2,1)} custom-call(s32[32]{0:T(128)S(1)} %stack.137.table, bf16[256,512]{1,0:T(8,128)(2,1)S(1)} %bitcast.46, bf16[1024,512]{1,0:T(8,128)(2,1)S(1)} %collective-permute-done.13.refs_0_, bf16[1024,512]{1,0:T(8,128)(2,1)S(1)} %collective-permute-done.15.refs_1_, ...), custom_call_target="tpu_custom_call" | custom-call | flops 1 | bytes 1 | tf_op jit(solution)/shard_map/pallas_call | solution.py:220
  81.9 2.8 %shard_map.138.refs_2_ = bf16[256,8192]{1,0:T(8,128)(2,1)} custom-call(s32[32]{0:T(128)S(1)} %stack.137.table, bf16[256,512]{1,0:T(8,128)(2,1)S(1)} %bitcast.47, bf16[1024,512]{1,0:T(8,128)(2,1)S(1)} %shard_map.132.refs_0_, bf16[1024,512]{1,0:T(8,128)(2,1)} %collective-permute-done.10.refs_1_, ...), custom_call_target="tpu_custom_call", output_to_operand_aliasing={{}: (4, {})} | custom-call | flops 1 | bytes 1 | tf_op jit(solution)/shard_map/pallas_call | solution.py:220
  84.8 2.4 %collective-permute-done.18.two = bf16[512,256]{1,0:T(8,128)(2,1)S(1)} collective-permute-done((bf16[512,256]{1,0:T(8,128)(2,1)S(1)}, bf16[512,256]{1,0:T(8,128)(2,1)S(1)}, u32[]{:S(2)}, u32[]{:S(2)}) %collective-permute-start.18) | collective-permute-done | bytes 262176 | tf_op jit(solution)/shard_map/rz_on/ppermute | solution.py:306
  87.2 1.3 %collective-permute-done.19.refs_0_ = bf16[1024,512]{1,0:T(8,128)(2,1)S(1)} collective-permute-done((bf16[1024,512]{1,0:T(8,128)(2,1)S(1)}, bf16[1024,512]{1,0:T(8,128)(2,1)S(1)}, u32[]{:S(2)}, u32[]{:S(2)}) %collective-permute-start.19) | collective-permute-done | bytes 1048608 | tf_op jit(solution)/shard_map/g_far/ppermute | solution.py:306
  88.5 2.6 %collective-permute-start.20 = (bf16[1024,512]{1,0:T(8,128)(2,1)S(1)}, bf16[1024,512]{1,0:T(8,128)(2,1)S(1)}, u32[]{:S(2)}, u32[]{:S(2)}) collective-permute-start(bf16[1024,512]{1,0:T(8,128)(2,1)S(1)} %collective-permute-done.19.refs_0_), channel_id=1, source_target_pairs={{0,1},{1,0},{2,3},{3,2},{4,5},{5,4},{6,7},{7,6},{8,9},{9,8},{10,11... | collective-permute-start | bytes 3145736 | tf_op jit(solution)/shard_map/swap_far/ppermute | solution.py:306
  91.1 2.1 %shard_map.139 = (f32[256,512]{1,0:T(8,128)}, f32[256,512]{1,0:T(8,128)}, f32[256,512]{1,0:T(8,128)}, f32[32,128]{1,0:T(8,128)}, f32[32,128]{1,0:T(8,128)}) custom-call(s32[2]{0:T(128)S(1)} %pad_add_fusion.place, bf16[512,256]{1,0:T(8,128)(2,1)S(1)} %get-tuple-element.194.own, bf16[512,256]{1,0:T(8,128)(2,1)S(1)} %collective-permute-done.17.one, ...), custom_call_target="tpu_custom_call" | custom-call | flops 1 | bytes 1 | tf_op jit(solution)/shard_map/pallas_call | solution.py:283
  93.2 0.1 collective-permute-done.20.refs_1_
  93.4 2.1 %shard_map.140 = bf16[256,8192]{1,0:T(8,128)(2,1)} custom-call(s32[32]{0:T(128)S(1)} %stack.137.table, bf16[256,512]{1,0:T(8,128)(2,1)S(1)} %bitcast.48, bf16[1024,512]{1,0:T(8,128)(2,1)S(1)} %collective-permute-done.19.refs_0_, bf16[1024,512]{1,0:T(8,128)(2,1)S(1)} %collective-permute-done.20.refs_1_, ...), custom_call_target="tpu_custom_call", output_to_operand_aliasing={{}: (4, {})} | custom-call | flops 1 | bytes 1 | tf_op jit(solution)/shard_map/pallas_call | solution.py:220
  (34 shorter events, 0.2 us)
Async XLA Ops:
  1.1 1.0 copy-start.1
  2.0 2.2 %copy-start.3 = (bf16[1,256,8192]{2,1,0:T(8,128)(2,1)S(1)}, bf16[1,256,8192]{2,1,0:T(8,128)(2,1)}, u32[]{:S(2)}) copy-start(bf16[1,256,8192]{2,1,0:T(8,128)(2,1)} %param.8) | copy-start | bytes 12582916
  5.4 11.3 %copy-start = (f32[1,256,512]{2,1,0:T(8,128)S(1)}, f32[1,256,512]{2,1,0:T(8,128)}, u32[]{:S(2)}) copy-start(f32[1,256,512]{2,1,0:T(8,128)} %param.10) | copy-start | bytes 1572868
  5.4 5.2 %collective-permute-start = (bf16[6,256,256]{2,1,0:T(8,128)(2,1)S(1)}, bf16[6,256,256]{2,1,0:T(8,128)(2,1)S(1)}, u32[]{:S(2)}, u32[]{:S(2)}) collective-permute-start(bf16[6,256,256]{2,1,0:T(8,128)(2,1)S(1)} %get-tuple-element.114), channel_id=1, source_target_pairs={{0,1},{1,0},{2,3},{3,2},{4,5},{5,4},{6,7},{7,6},{8,9},{9,8},{10,11... | collective-permute-start | bytes 2359304 | tf_op jit(solution)/shard_map/swap_inputs/ppermute | solution.py:306
  10.6 3.4 %collective-permute-start.1 = (bf16[12,256,256]{2,1,0:T(8,128)(2,1)S(1)}, bf16[12,256,256]{2,1,0:T(8,128)(2,1)S(1)}, u32[]{:S(2)}, u32[]{:S(2)}) collective-permute-start(bf16[12,256,256]{2,1,0:T(8,128)(2,1)S(1)} %get-tuple-element.121), channel_id=1, source_target_pairs={{0,1},{1,0},{2,3},{3,2},{4,5},{5,4},{6,7},{7,6},{8,9},{9,8},{10,11... | collective-permute-start | bytes 4718600 | tf_op jit(solution)/shard_map/swap_inputs_late/ppermute | solution.py:306
  11.7 20.6 %collective-permute-start.4 = (bf16[4,512,256]{2,1,0:T(8,128)(2,1)S(1)}, bf16[4,512,256]{2,1,0:T(8,128)(2,1)S(1)}, u32[]{:S(2)}, u32[]{:S(2)}) collective-permute-start(bf16[4,512,256]{2,1,0:T(8,128)(2,1)S(1)} %shard_map.128), channel_id=1, source_target_pairs={{0,2},{1,7},{2,4},{3,1},{4,6},{5,3},{6,0},{7,5},{8,10},{9,15},{10,... | collective-permute-start | bytes 3145736 | tf_op jit(solution)/shard_map/r_far/ppermute | solution.py:306
  16.7 25.1 %copy-start.4 = (bf16[4,512,256]{2,1,0:T(8,128)(2,1)}, bf16[4,512,256]{2,1,0:T(8,128)(2,1)S(1)}, u32[]{:S(2)}) copy-start(bf16[4,512,256]{2,1,0:T(8,128)(2,1)S(1)} %get-tuple-element.153.refs_0_) | copy-start | bytes 3145732
  16.7 28.6 %copy-start.8 = (f32[32,128]{1,0:T(8,128)S(1)}, f32[32,128]{1,0:T(8,128)}, u32[]{:S(2)}) copy-start(f32[32,128]{1,0:T(8,128)} %outer.3) | copy-start | bytes 49156
  16.7 28.6 %copy-start.9 = (f32[32,128]{1,0:T(8,128)S(1)}, f32[32,128]{1,0:T(8,128)}, u32[]{:S(2)}) copy-start(f32[32,128]{1,0:T(8,128)} %momentum.3) | copy-start | bytes 49156
  16.7 28.6 %collective-permute-start.6 = (bf16[4,512,256]{2,1,0:T(8,128)(2,1)}, bf16[4,512,256]{2,1,0:T(8,128)(2,1)}, u32[]{:S(2)}, u32[]{:S(2)}) collective-permute-start(bf16[4,512,256]{2,1,0:T(8,128)(2,1)} %get-tuple-element.144), channel_id=1, source_target_pairs={{0,6},{1,3},{2,0},{3,5},{4,2},{5,7},{6,4},{7,1},{8,14},{9,11},{10,... | collective-permute-start | bytes 3145736 | tf_op jit(solution)/shard_map/r_back/ppermute | solution.py:306
  16.7 10.1 %collective-permute-start.2 = (bf16[256,512]{1,0:T(8,128)(2,1)S(1)}, bf16[256,512]{1,0:T(8,128)(2,1)S(1)}, u32[]{:S(2)}, u32[]{:S(2)}) collective-permute-start(bf16[256,512]{1,0:T(8,128)(2,1)S(1)} %shard_map.130.refs_0_), channel_id=1, source_target_pairs={{0,8},{1,25},{2,10},{3,27},{4,12},{5,29},{6,14},{7,31},{8,16},{9,1... | collective-permute-start | bytes 786440 | tf_op jit(solution)/shard_map/z_on/ppermute | solution.py:306
  20.7 11.7 %collective-permute-start.3 = (bf16[256,512]{1,0:T(8,128)(2,1)S(1)}, bf16[256,512]{1,0:T(8,128)(2,1)S(1)}, u32[]{:S(2)}, u32[]{:S(2)}) collective-permute-start(bf16[256,512]{1,0:T(8,128)(2,1)S(1)} %shard_map.130.refs_0_), channel_id=1, source_target_pairs={{0,24},{1,9},{2,26},{3,11},{4,28},{5,13},{6,30},{7,15},{8,0},{9,17... | collective-permute-start | bytes 786440 | tf_op jit(solution)/shard_map/z_back/ppermute | solution.py:306
  32.4 9.2 %collective-permute-start.5 = (bf16[256,512]{1,0:T(8,128)(2,1)S(1)}, bf16[256,512]{1,0:T(8,128)(2,1)S(1)}, u32[]{:S(2)}, u32[]{:S(2)}) collective-permute-start(bf16[256,512]{1,0:T(8,128)(2,1)S(1)} %collective-permute-done.2.refs_1_), channel_id=1, source_target_pairs={{0,8},{1,25},{2,10},{3,27},{4,12},{5,29},{6,14},{7,31},{8,16},{9,1... | collective-permute-start | bytes 786440 | tf_op jit(solution)/shard_map/z_far/ppermute | solution.py:306
  33.6 25.1 %collective-permute-start.9 = (bf16[4,512,256]{2,1,0:T(8,128)(2,1)}, bf16[4,512,256]{2,1,0:T(8,128)(2,1)}, u32[]{:S(2)}, u32[]{:S(2)}) collective-permute-start(bf16[4,512,256]{2,1,0:T(8,128)(2,1)} %shard_map.131), channel_id=1, source_target_pairs={{0,2},{1,7},{2,4},{3,1},{4,6},{5,3},{6,0},{7,5},{8,10},{9,15},{10,... | collective-permute-start | bytes 3145736 | tf_op jit(solution)/shard_map/r_on/ppermute | solution.py:306
  41.6 36.9 %copy-start.2 = (bf16[1,256,512]{2,1,0:T(8,128)(2,1)S(1)}, bf16[1,256,512]{2,1,0:T(8,128)(2,1)}, u32[]{:S(2)}) copy-start(bf16[1,256,512]{2,1,0:T(8,128)(2,1)} %param.9) | copy-start | bytes 786436
  41.6 22.0 %collective-permute-start.10 = (bf16[1024,512]{1,0:T(8,128)(2,1)S(1)}, bf16[1024,512]{1,0:T(8,128)(2,1)}, u32[]{:S(2)}, u32[]{:S(2)}) collective-permute-start(bf16[1024,512]{1,0:T(8,128)(2,1)S(1)} %shard_map.132.refs_0_), channel_id=1, source_target_pairs={{0,1},{1,0},{2,3},{3,2},{4,5},{5,4},{6,7},{7,6},{8,9},{9,8},{10,11... | collective-permute-start | bytes 3145736 | tf_op jit(solution)/shard_map/swap_near/ppermute | solution.py:306
  41.8 28.3 %collective-permute-start.14 = (bf16[1024,512]{1,0:T(8,128)(2,1)S(1)}, bf16[1024,512]{1,0:T(8,128)(2,1)}, u32[]{:S(2)}, u32[]{:S(2)}) collective-permute-start(bf16[1024,512]{1,0:T(8,128)(2,1)S(1)} %shard_map.132.refs_0_), channel_id=1, source_target_pairs={{0,6},{1,3},{2,0},{3,5},{4,2},{5,7},{6,4},{7,1},{8,14},{9,11},{10,... | collective-permute-start | bytes 3145736 | tf_op jit(solution)/shard_map/g_back/ppermute | solution.py:306
  43.5 29.0 %collective-permute-start.13 = (bf16[1024,512]{1,0:T(8,128)(2,1)S(1)}, bf16[1024,512]{1,0:T(8,128)(2,1)S(1)}, u32[]{:S(2)}, u32[]{:S(2)}) collective-permute-start(bf16[1024,512]{1,0:T(8,128)(2,1)S(1)} %shard_map.132.refs_0_), channel_id=1, source_target_pairs={{0,2},{1,7},{2,4},{3,1},{4,6},{5,3},{6,0},{7,5},{8,10},{9,15},{10,... | collective-permute-start | bytes 3145736 | tf_op jit(solution)/shard_map/g_on/ppermute | solution.py:306
  46.0 7.9 %collective-permute-start.7 = (bf16[256,128]{1,0:T(8,128)(2,1)S(1)}, bf16[256,128]{1,0:T(8,128)(2,1)S(1)}, u32[]{:S(2)}, u32[]{:S(2)}) collective-permute-start(bf16[256,128]{1,0:T(8,128)(2,1)S(1)} %convert_element_type.6), channel_id=1, source_target_pairs={{0,128},{32,160},{64,192},{96,224},{128,0},{160,32},{192,64},{224,... | collective-permute-start | bytes 196616 | tf_op jit(solution)/shard_map/frag_h/ppermute | solution.py:310
  53.9 4.8 %collective-permute-start.8 = (f32[256,128]{1,0:T(8,128)S(1)}, f32[256,128]{1,0:T(8,128)S(1)}, u32[]{:S(2)}, u32[]{:S(2)}) collective-permute-start(f32[256,128]{1,0:T(8,128)S(1)} %convert_add_fusion), channel_id=1, source_target_pairs={{0,32},{32,0},{64,96},{96,64},{128,160},{160,128},{192,224},{224,1... | collective-permute-start | bytes 393224 | tf_op jit(solution)/shard_map/frag_x1/ppermute | solution.py:310
  55.4 1.2 %copy-start.5 = (bf16[4,512,256]{2,1,0:T(8,128)(2,1)S(1)}, bf16[4,512,256]{2,1,0:T(8,128)(2,1)}, u32[]{:S(2)}) copy-start(bf16[4,512,256]{2,1,0:T(8,128)(2,1)} %copy-done.4) | copy-start | bytes 3145732
  60.2 9.9 %collective-permute-start.12 = (bf16[512,256]{1,0:T(8,128)(2,1)S(1)}, bf16[512,256]{1,0:T(8,128)(2,1)S(1)}, u32[]{:S(2)}, u32[]{:S(2)}) collective-permute-start(bf16[512,256]{1,0:T(8,128)(2,1)S(1)} %get-tuple-element.175), channel_id=1, source_target_pairs={{0,8},{1,25},{2,10},{3,27},{4,12},{5,29},{6,14},{7,31},{8,16},{9,1... | collective-permute-start | bytes 786440 | tf_op jit(solution)/shard_map/rz_far/ppermute | solution.py:306
  61.2 5.3 %collective-permute-start.11 = (f32[256,128]{1,0:T(8,128)S(1)}, f32[256,128]{1,0:T(8,128)S(1)}, u32[]{:S(2)}, u32[]{:S(2)}) collective-permute-start(f32[256,128]{1,0:T(8,128)S(1)} %add.487), channel_id=1, source_target_pairs={{0,96},{32,64},{64,32},{96,0},{128,224},{160,192},{192,160},{224,1... | collective-permute-start | bytes 393224 | tf_op jit(solution)/shard_map/frag_x2/ppermute | solution.py:310
  72.4 6.1 %collective-permute-start.16 = (bf16[1024,512]{1,0:T(8,128)(2,1)}, bf16[1024,512]{1,0:T(8,128)(2,1)S(1)}, u32[]{:S(2)}, u32[]{:S(2)}) collective-permute-start(bf16[1024,512]{1,0:T(8,128)(2,1)} %collective-permute-done.14.refs_2_), channel_id=1, source_target_pairs={{0,1},{1,0},{2,3},{3,2},{4,5},{5,4},{6,7},{7,6},{8,9},{9,8},{10,11... | collective-permute-start | bytes 3145736 | tf_op jit(solution)/shard_map/swap_back/ppermute | solution.py:306
  74.5 4.0 %collective-permute-start.15 = (bf16[1024,512]{1,0:T(8,128)(2,1)S(1)}, bf16[1024,512]{1,0:T(8,128)(2,1)S(1)}, u32[]{:S(2)}, u32[]{:S(2)}) collective-permute-start(bf16[1024,512]{1,0:T(8,128)(2,1)S(1)} %collective-permute-done.13.refs_0_), channel_id=1, source_target_pairs={{0,1},{1,0},{2,3},{3,2},{4,5},{5,4},{6,7},{7,6},{8,9},{9,8},{10,11... | collective-permute-start | bytes 3145736 | tf_op jit(solution)/shard_map/swap_on/ppermute | solution.py:306
  74.5 13.9 %collective-permute-start.19 = (bf16[1024,512]{1,0:T(8,128)(2,1)S(1)}, bf16[1024,512]{1,0:T(8,128)(2,1)S(1)}, u32[]{:S(2)}, u32[]{:S(2)}) collective-permute-start(bf16[1024,512]{1,0:T(8,128)(2,1)S(1)} %collective-permute-done.13.refs_0_), channel_id=1, source_target_pairs={{0,2},{1,7},{2,4},{3,1},{4,6},{5,3},{6,0},{7,5},{8,10},{9,15},{10,... | collective-permute-start | bytes 3145736 | tf_op jit(solution)/shard_map/g_far/ppermute | solution.py:306
  74.9 9.9 %collective-permute-start.17 = (bf16[512,256]{1,0:T(8,128)(2,1)S(1)}, bf16[512,256]{1,0:T(8,128)(2,1)S(1)}, u32[]{:S(2)}, u32[]{:S(2)}) collective-permute-start(bf16[512,256]{1,0:T(8,128)(2,1)S(1)} %get-tuple-element.190), channel_id=1, source_target_pairs={{0,24},{1,9},{2,26},{3,11},{4,28},{5,13},{6,30},{7,15},{8,0},{9,17... | collective-permute-start | bytes 786440 | tf_op jit(solution)/shard_map/rz_back/ppermute | solution.py:306
  75.5 11.7 %collective-permute-start.18 = (bf16[512,256]{1,0:T(8,128)(2,1)S(1)}, bf16[512,256]{1,0:T(8,128)(2,1)S(1)}, u32[]{:S(2)}, u32[]{:S(2)}) collective-permute-start(bf16[512,256]{1,0:T(8,128)(2,1)S(1)} %shard_map.136), channel_id=1, source_target_pairs={{0,8},{1,25},{2,10},{3,27},{4,12},{5,29},{6,14},{7,31},{8,16},{9,1... | collective-permute-start | bytes 786440 | tf_op jit(solution)/shard_map/rz_on/ppermute | solution.py:306
  81.9 9.2 %copy-start.6 = (f32[1,256,512]{2,1,0:T(8,128)S(1)}, f32[1,256,512]{2,1,0:T(8,128)}, u32[]{:S(2)}) copy-start(f32[1,256,512]{2,1,0:T(8,128)} %param.11) | copy-start | bytes 1572868
  81.9 9.2 %copy-start.7 = (f32[1,256,512]{2,1,0:T(8,128)S(1)}, f32[1,256,512]{2,1,0:T(8,128)}, u32[]{:S(2)}) copy-start(f32[1,256,512]{2,1,0:T(8,128)} %param.12) | copy-start | bytes 1572868
  88.5 4.9 %collective-permute-start.20 = (bf16[1024,512]{1,0:T(8,128)(2,1)S(1)}, bf16[1024,512]{1,0:T(8,128)(2,1)S(1)}, u32[]{:S(2)}, u32[]{:S(2)}) collective-permute-start(bf16[1024,512]{1,0:T(8,128)(2,1)S(1)} %collective-permute-done.19.refs_0_), channel_id=1, source_target_pairs={{0,1},{1,0},{2,3},{3,2},{4,5},{5,4},{6,7},{7,6},{8,9},{9,8},{10,11... | collective-permute-start | bytes 3145736 | tf_op jit(solution)/shard_map/swap_far/ppermute | solution.py:306
